TPU v7x, 32 devices: a whole 2x2x4 slice. The times are simulated.
32 devices in a mesh: dp: 4 (over x, core), mp: 8 (over z, y).
Axes of the slice: x: 2, y: 2, z: 4, core: 2. Of those that a mesh axis runs over, the one named last changes fastest.
Arguments:
- fields: float32 [4, 32, 128, 128, 128], P('dp', None, 'mp'), may hold values from -6 to 6
- upstream: bfloat16 [4, 32, 128, 128, 128], P('dp', None, 'mp'), may hold values from -6 to 6
- spectral_weight: float32 [2, 32, 32, 32, 1024], P(None, None, None, 'dp', 'mp'), may hold values from -4.2 to 4.2
- point_weight: float32 [32, 32], replicated, may hold values from -1 to 1
- point_bias: float32 [32], replicated, may hold values from -3 to 3
Outputs:
- grad_fields: float32 [4, 32, 128, 128, 128], P('dp', None, 'mp')
- grad_weight: float32 [2, 32, 32, 32, 1024], P(None, None, None, 'dp', 'mp')
All inputs are finite; a program needn't handle non-finite values.
Results may differ from a plain program's by a relative error of at most 0.0003.
Values sent between devices are 32-bit elements; how exact they have to be, the bound alone decides.
No kernel may reach another device: no remote copies, remote signals or barrier semaphores. Data moves between devices by JAX's collectives and lax.ppermute only.
A program may use at most 320 MiB of HBM per device.

v0:
```python
from functools import partial
import math

import jax
import jax.numpy as jnp
from jax import lax
from jax.sharding import PartitionSpec as P

NX = 128
NY = 128
NZ = 128
MX = 32
MY = 32
MZ = 32


HIGHEST = lax.Precision.HIGHEST


def tables(number, kept_modes, signed):
    positions = jnp.arange(number, dtype=jnp.int32)
    frequency = jnp.arange(kept_modes, dtype=jnp.int32)
    if signed:
        frequency = jnp.where(frequency < kept_modes // 2, frequency, frequency - kept_modes)
    phases = jnp.mod(positions[:, None] * frequency[None, :], number).astype(jnp.float32) * (
        2.0 * math.pi / number
    )
    return jnp.concatenate([jnp.cos(phases), jnp.sin(phases)], axis=1)


def forward_plane(grid_field, table_y, table_z):
    along_y = jnp.einsum("scpyz,yj->scpjz", grid_field, table_y, precision=HIGHEST)
    products = jnp.einsum("scpjz,zk->scpjk", along_y, table_z, precision=HIGHEST)
    cos_cos = products[:, :, :, :MY, :MZ]
    cos_sin = products[:, :, :, :MY, MZ:]
    sin_cos = products[:, :, :, MY:, :MZ]
    sin_sin = products[:, :, :, MY:, MZ:]
    result = jnp.stack([cos_cos - sin_sin, -(sin_cos + cos_sin)], axis=3)
    return result.reshape(result.shape[:4] + (MY * MZ,))


def forward_line(pieces, table_x):
    products = jnp.einsum("scxrm,xk->scrkm", pieces, table_x, precision=HIGHEST)
    real_part = products[:, :, 0, :MX] + products[:, :, 1, MX:]
    imag_part = products[:, :, 1, :MX] - products[:, :, 0, MX:]
    return jnp.stack([real_part, imag_part], axis=2)


def inverse_line(spectrum, table_x):
    real_part = spectrum[:, :, 0]
    imag_part = spectrum[:, :, 1]
    stacked = jnp.stack(
        [
            jnp.concatenate([real_part, -imag_part], axis=2),
            jnp.concatenate([imag_part, real_part], axis=2),
        ],
        axis=2,
    )
    return jnp.einsum("scrjm,xj->scxrm", stacked, table_x, precision=HIGHEST)


def inverse_plane(pieces, table_y, table_z):
    shaped = pieces.reshape(pieces.shape[:4] + (MY, MZ))
    real_part = shaped[:, :, :, 0]
    imag_part = shaped[:, :, :, 1]
    stacked = jnp.stack(
        [
            jnp.concatenate([real_part, -imag_part], axis=3),
            jnp.concatenate([imag_part, real_part], axis=3),
        ],
        axis=3,
    )
    along_y = jnp.einsum("scpwjk,yj->scpwyk", stacked, table_y, precision=HIGHEST)
    merged = jnp.concatenate([along_y[:, :, :, 0], -along_y[:, :, :, 1]], axis=4)
    return jnp.einsum("scpyj,zj->scpyz", merged, table_z, precision=HIGHEST)


def mix_forward(weight, spectrum):
    real_weight = weight[0]
    imag_weight = weight[1]
    real_spec = spectrum[:, :, 0]
    imag_spec = spectrum[:, :, 1]
    real_part = jnp.einsum(
        "sixm,ioxm->soxm", real_spec, real_weight, precision=HIGHEST
    ) - jnp.einsum("sixm,ioxm->soxm", imag_spec, imag_weight, precision=HIGHEST)
    imag_part = jnp.einsum(
        "sixm,ioxm->soxm", imag_spec, real_weight, precision=HIGHEST
    ) + jnp.einsum("sixm,ioxm->soxm", real_spec, imag_weight, precision=HIGHEST)
    return jnp.stack([real_part, imag_part], axis=2)


def mix_adjoint(weight, gradient):
    real_weight = weight[0]
    imag_weight = weight[1]
    real_grad = gradient[:, :, 0]
    imag_grad = gradient[:, :, 1]
    real_part = jnp.einsum(
        "soxm,ioxm->sixm", real_grad, real_weight, precision=HIGHEST
    ) + jnp.einsum("soxm,ioxm->sixm", imag_grad, imag_weight, precision=HIGHEST)
    imag_part = jnp.einsum(
        "soxm,ioxm->sixm", imag_grad, real_weight, precision=HIGHEST
    ) - jnp.einsum("soxm,ioxm->sixm", real_grad, imag_weight, precision=HIGHEST)
    return jnp.stack([real_part, imag_part], axis=2)


def weight_gradient(gradient, spectrum):
    real_grad = gradient[:, :, 0]
    imag_grad = gradient[:, :, 1]
    real_spec = spectrum[:, :, 0]
    imag_spec = spectrum[:, :, 1]
    real_part = jnp.einsum("soxm,sixm->ioxm", real_grad, real_spec, precision=HIGHEST) + jnp.einsum(
        "soxm,sixm->ioxm", imag_grad, imag_spec, precision=HIGHEST
    )
    imag_part = jnp.einsum("soxm,sixm->ioxm", imag_grad, real_spec, precision=HIGHEST) - jnp.einsum(
        "soxm,sixm->ioxm", real_grad, imag_spec, precision=HIGHEST
    )
    return jnp.stack([real_part, imag_part], axis=0)


def shards(fields, upstream, spectral_weight, point_weight, point_bias):
    table_y = tables(NY, MY, True)
    table_z = tables(NZ, MZ, False)
    table_x = tables(NX, MX, True)
    modes_dev = spectral_weight.shape[4]
    mode_index = lax.axis_index("mp") * modes_dev + jnp.arange(modes_dev, dtype=jnp.int32)
    kz_index = jnp.mod(mode_index, MZ)
    factor = jnp.where(kz_index == 0, 1.0, 2.0).astype(jnp.float32) / float(NX * NY * NZ)

    def to_modes(pieces):
        return forward_line(pieces, table_x)

    def to_cells(pieces):
        return inverse_plane(pieces, table_y, table_z)

    spectrum = to_modes(
        lax.all_to_all(
            forward_plane(fields, table_y, table_z), "mp", split_axis=4, concat_axis=2, tiled=True
        )
    )
    full_weight = lax.all_gather(spectral_weight, "dp", axis=3, tiled=True)
    mixed_spec = mix_forward(full_weight, spectrum)
    mixed_spec = mixed_spec * factor
    spectral_part = to_cells(
        lax.all_to_all(
            inverse_line(mixed_spec, table_x), "mp", split_axis=2, concat_axis=4, tiled=True
        )
    )
    preact = spectral_part + jnp.einsum("scpyz,co->sopyz", fields, point_weight, precision=HIGHEST)
    preact = preact + point_bias[None, :, None, None, None]
    activation, pullback = jax.vjp(partial(jax.nn.gelu, approximate=False), preact)
    grad_pre = pullback(upstream.astype(jnp.float32))[0]
    grad_spec = to_modes(
        lax.all_to_all(
            forward_plane(grad_pre, table_y, table_z), "mp", split_axis=4, concat_axis=2, tiled=True
        )
    )
    grad_spec = grad_spec * factor
    back_spec = mix_adjoint(full_weight, grad_spec)
    weight_out = lax.psum_scatter(
        weight_gradient(grad_spec, spectrum), "dp", scatter_dimension=3, tiled=True
    )
    spectral_back = to_cells(
        lax.all_to_all(
            inverse_line(back_spec, table_x), "mp", split_axis=2, concat_axis=4, tiled=True
        )
    )
    grad_fields = spectral_back + jnp.einsum(
        "sopyz,co->scpyz", grad_pre, point_weight, precision=HIGHEST
    )
    return (grad_fields, weight_out)


def solution(mesh):
    placed = (
        P("dp", None, "mp", None, None),
        P("dp", None, "mp", None, None),
        P(None, None, None, "dp", "mp"),
        P(),
        P(),
    )
    return jax.shard_map(
        shards,
        mesh=mesh,
        in_specs=placed,
        out_specs=(P("dp", None, "mp", None, None), P(None, None, None, "dp", "mp")),
        check_vma=False,
    )
```

profile of v0, /device:TPU:0, one launch (start us, length us, event | category | flops | bytes accessed | tf_op | source)
XLA Modules:
  0.0 1188.7 jit_solution(10635163593331632130)
XLA Ops:
  8.2 25.3 %fusion.76 = f32[64,32,16,128]{3,0,2,1:T(8,128)S(1)} fusion(f32[1,32,16,128,128]{4,3,2,1,0:T(8,128)} %param.5, f32[128,32]{0,1:T(8,128)S(1)} %get-tuple-element.47, f32[128,32]{0,1:T(8,128)S(1)} %get-tuple-element.46), kind=kOutput, calls=%fused_computation.139 | convolution fusion | flops 6442459136 | bytes 50364416 | tf_op jit(solution)/shard_map/scpyz,yj->scpjz/dot_general | solution.py:32
  33.5 15.7 %fusion.46 = f32[1,32,16,64,64]{4,3,2,1,0:T(8,128)} fusion(f32[64,32,16,128]{3,0,2,1:T(8,128)S(1)} %fusion.76, f32[128,32]{0,1:T(8,128)S(1)} %get-tuple-element.48, f32[128,32]{0,1:T(8,128)S(1)} %get-tuple-element.49), kind=kOutput, calls=%fused_computation.76 | convolution fusion | flops 3221233664 | bytes 25198592 | tf_op jit(solution)/shard_map/scpjz,zk->scpjk/dot_general | solution.py:33
  49.2 20.2 %slice_subtract_fusion.1 = (f32[1,32,16,32,32]{4,3,2,1,0:T(8,128)}, f32[1,32,16,32,32]{4,3,2,1,0:T(8,128)}) fusion(f32[1,32,16,64,64]{4,3,2,1,0:T(8,128)} %fusion.46), kind=kLoop, calls=%fused_computation.91 | loop fusion | flops 1572864 | bytes 12582912 | tf_op jit(solution)/shard_map/sub | solution.py:38
  69.3 10.9 copy.184
  80.3 10.7 copy.185
  91.0 20.7 %fusion.113 = f32[1024,1,2,16,32]{4,3,2,1,0:T(8,128)} fusion(f32[1,32,16,1,1024]{1,2,3,0,4:T(8,128)} %bitcast.335, f32[1,32,16,1,1024]{1,2,3,0,4:T(8,128)} %bitcast.333), kind=kLoop, calls=%fused_computation.189 | loop fusion | flops 1048576 | bytes 8388608
  111.7 12.8 %reshape.417 = f32[8,1,131072]{2,1,0:T(1,128)} reshape(f32[1024,1,2,16,32]{4,3,2,1,0:T(8,128)} %fusion.113) | data formatting | bytes 8388608
  124.5 7.9 all-to-all-start
  132.3 93.2 %all-to-all-done = f32[8,1,131072]{2,1,0:T(1,128)} async-done(((f32[8,1,131072]{2,1,0:T(1,128)}), f32[8,1,131072]{2,1,0:T(1,128)}, u32[]{:S(2)}, u32[]{:S(2)}) %all-to-all-start) | async-done | bytes 4194336 | tf_op jit(solution)/shard_map/all_to_all | solution.py:136
  226.1 13.7 %reduce.16 = f32[8,131072]{1,0:T(8,128)} reduce(f32[8,1,131072]{2,1,0:T(1,128)} %all-to-all-done, f32[]{:T(128)} %broadcast.196), dimensions={1}, to_apply=%all_to_all.44.reduce_sub_computation | reduce | bytes 8388612 | tf_op jit(solution)/shard_map/all_to_all | solution.py:136
  239.7 13.8 %reshape.418 = f32[1024,1,2,16,32]{4,3,2,1,0:T(8,128)} reshape(f32[8,131072]{1,0:T(8,128)} %reduce.16) | data formatting | bytes 8388608
  253.5 13.1 %copy.97 = f32[1,32,16,2,8,128]{5,2,4,3,1,0:T(8,128)} copy(f32[1,32,16,2,8,128]{1,2,3,5,4,0:T(8,128)} %bitcast.329) | data formatting | bytes 8388608 | tf_op jit(solution)/shard_map/all_to_all | solution.py:136
  270.9 13.0 %fusion.42 = (f32[32,128,32]{1,0,2:T(8,128)S(1)}, f32[32,128,32]{1,0,2:T(8,128)S(1)}, f32[32,128,32]{1,0,2:T(8,128)S(1)}, f32[32,128,32]{1,0,2:T(8,128)S(1)}) fusion(f32[2,32,32,32,128]{4,3,2,1,0:T(8,128)} %all-gather.2.cloned.1.call-done, f32[32,128,32]{1,0,2:T(8,128)S(1)} %get-tuple-element.37, f32[32,128,32]{1,0,2:T(8,128)S(1)} %get-tuple-element.36), kind=kLoop, calls=%fused_computation.68 | loop fusion | flops 33030144 | bytes 36700160 | tf_op jit(solution)/shard_map/sixm,ioxm->soxm/dot_general | solution.py:85
  298.0 56.8 %fusion.13 = f32[32,16,128,128]{3,0,2,1:T(8,128)} fusion(f32[32,16,128,128]{3,2,1,0:T(8,128)} %bitcast.326, f32[32,32]{1,0:T(8,128)S(1)} %copy-done), kind=kOutput, calls=%fused_computation.19 | convolution fusion | flops 3221225472 | bytes 67112960 | tf_op jit(solution)/shard_map/scpyz,co->sopyz/dot_general | solution.py:148
  354.8 35.7 %all-to-all-done.1 = f32[1,32,128,2,128]{4,3,1,0,2:T(2,128)} async-done(((f32[1,32,128,2,128]{4,3,1,0,2:T(2,128)}), f32[1,32,128,2,128]{4,3,1,0,2:T(2,128)}, u32[]{:S(2)}, u32[]{:S(2)}) %all-to-all-start.1) | async-done | bytes 4194336 | tf_op jit(solution)/shard_map/all_to_all | solution.py:144
  397.1 10.9 reshape.384
  408.0 11.0 fusion.111
  419.0 9.1 copy.190
  428.1 8.4 bitcast_negate_fusion.1
  436.5 9.0 copy.189
  445.4 16.3 %maximum_bitcast_fusion.14 = (f32[1,32,16,1,64,32]{4,5,3,2,1,0:T(8,128)}, f32[1,32,16,1,64,32]{4,5,3,2,1,0:T(8,128)}) fusion(f32[1,32,16,32,32]{3,4,2,1,0:T(8,128)} %bitcast_negate_fusion.1, f32[1,32,16,32,32]{3,4,2,1,0:T(8,128)} %bitcast.331, f32[1,32,16,32,32]{3,4,2,1,0:T(8,128)} %bitcast.327), kind=kLoop, calls=%fused_computation.92 | loop fusion | flops 2097152 | bytes 14680064 | tf_op jit(solution)/shard_map/stack | solution.py:66
  461.7 17.2 %fusion.53 = f32[1,32,16,2,128,32]{4,5,3,2,1,0:T(8,128)S(1)} fusion(f32[1,32,16,1,64,32]{4,5,3,2,1,0:T(8,128)} %get-tuple-element.31, f32[1,32,16,1,64,32]{4,5,3,2,1,0:T(8,128)} %get-tuple-element.30, f32[128,32]{0,1:T(8,128)S(1)} %get-tuple-element.47, f32[128,32]{0,1:T(8,128)S(1)} %get-tuple-element.46), kind=kOutput, calls=%fused_computation.79 | convolution fusion | flops 3223330816 | bytes 25198592 | tf_op jit(solution)/shard_map/scpwjk,yj->scpwyk/dot_general | solution.py:73
  478.9 6.9 slice_bitcast_fusion.1
  485.9 59.0 %fusion.25 = f32[32,16,128,128]{3,2,1,0:T(8,128)} fusion(f32[1,32,16,128,32]{3,4,2,1,0:T(8,128)} %get-tuple-element.23, f32[1,32,16,128,32]{3,4,2,1,0:T(8,128)} %get-tuple-element.22, f32[128,32]{0,1:T(8,128)S(1)} %copy-done.6, f32[128,32]{0,1:T(8,128)S(1)} %copy-done.9), kind=kOutput, calls=%fused_computation.42 | convolution fusion | flops 6446653440 | bytes 50364416 | tf_op jit(solution)/shard_map/scpyj,zj->scpyz/dot_general | solution.py:75
  544.9 87.5 %fusion.5 = f32[32,16,128,128]{3,2,1,0:T(8,128)} fusion(bf16[1,32,16,128,128]{4,3,2,1,0:T(8,128)(2,1)} %param.6, f32[32,16,128,128]{3,2,1,0:T(8,128)} %fusion.25, f32[32,16,128,128]{3,0,2,1:T(8,128)} %fusion.13, f32[32]{0:T(128)S(1)} %copy-done.13), kind=kLoop, calls=%fused_computation.8 | loop fusion | flops 620756992 | bytes 117440640 | tf_op jit(solution)/shard_map/reshape.32
  632.4 25.3 %fusion.72 = f32[64,32,16,128]{3,0,2,1:T(8,128)S(1)} fusion(f32[32,16,128,128]{3,2,1,0:T(8,128)} %fusion.5, f32[128,32]{0,1:T(8,128)S(1)} %get-tuple-element.47, f32[128,32]{0,1:T(8,128)S(1)} %get-tuple-element.46), kind=kOutput, calls=%fused_computation.135 | convolution fusion | flops 6442459136 | bytes 50364416 | tf_op jit(solution)/shard_map/scpyz,yj->scpjz/dot_general | solution.py:32
  657.7 15.7 %fusion.49 = f32[1,32,16,64,64]{4,3,2,1,0:T(8,128)} fusion(f32[64,32,16,128]{3,0,2,1:T(8,128)S(1)} %fusion.72, f32[128,32]{0,1:T(8,128)S(1)} %copy-done.6, f32[128,32]{0,1:T(8,128)S(1)} %copy-done.9), kind=kOutput, calls=%fused_computation.77 | convolution fusion | flops 3221233664 | bytes 25198592 | tf_op jit(solution)/shard_map/scpjz,zk->scpjk/dot_general | solution.py:33
  673.5 19.6 %slice_subtract_fusion = (f32[1,32,16,32,32]{4,3,2,1,0:T(8,128)}, f32[1,32,16,32,32]{4,3,2,1,0:T(8,128)}) fusion(f32[1,32,16,64,64]{4,3,2,1,0:T(8,128)} %fusion.49), kind=kLoop, calls=%fused_computation.85 | loop fusion | flops 1572864 | bytes 12582912 | tf_op jit(solution)/shard_map/sub | solution.py:38
  693.0 10.8 copy.187
  703.8 10.7 copy.188
  714.5 11.6 fusion.112
  726.1 12.8 %reshape.419 = f32[8,1,131072]{2,1,0:T(1,128)} reshape(f32[1024,1,2,16,32]{4,3,2,1,0:T(8,128)} %fusion.112) | data formatting | bytes 8388608
  738.9 97.7 %all_to_all.60 = f32[8,1,131072]{2,1,0:T(1,128)} all-to-all(f32[8,1,131072]{2,1,0:T(1,128)} %reshape.419), channel_id=1, replica_groups=mesh['dp'=4,'mp'=8] {'mp'}, dimensions={0} | all-to-all | bytes 8388608 | tf_op jit(solution)/shard_map/all_to_all | solution.py:153
  836.6 13.7 %reduce.17 = f32[8,131072]{1,0:T(8,128)} reduce(f32[8,1,131072]{2,1,0:T(1,128)} %all_to_all.60, f32[]{:T(128)} %broadcast.196), dimensions={1}, to_apply=%all_to_all.50.reduce_sub_computation | reduce | bytes 8388612 | tf_op jit(solution)/shard_map/all_to_all | solution.py:153
  850.3 13.3 %reshape.420 = f32[1024,1,2,16,32]{4,3,2,1,0:T(8,128)} reshape(f32[8,131072]{1,0:T(8,128)} %reduce.17) | data formatting | bytes 8388608
  863.6 13.2 %copy.110 = f32[1,32,16,2,8,128]{5,2,4,3,1,0:T(8,128)} copy(f32[1,32,16,2,8,128]{1,2,3,5,4,0:T(8,128)} %bitcast.330) | data formatting | bytes 8388608 | tf_op jit(solution)/shard_map/all_to_all | solution.py:153
  887.1 11.6 pad_maximum_fusion
  898.7 17.9 %fusion.39 = (f32[32,128,32]{1,0,2:T(8,128)S(1)}, f32[32,128,32]{1,0,2:T(8,128)S(1)}, f32[32,128,32]{1,0,2:T(8,128)S(1)}, f32[32,128,32]{1,0,2:T(8,128)S(1)}) fusion(f32[2,32,32,32,128]{4,3,2,1,0:T(8,128)} %all-gather.2.cloned.1.call-done, f32[32,128,32]{1,0,2:T(8,128)S(1)} %get-tuple-element.39, f32[32,128,32]{1,0,2:T(8,128)S(1)} %get-tuple-element.38), kind=kLoop, calls=%fused_computation.61 | loop fusion | flops 33030144 | bytes 36700160 | tf_op jit(solution)/shard_map/soxm,ioxm->sixm/dot_general | solution.py:102
  931.0 61.9 %fusion.10 = f32[16,128,128,32]{2,3,1,0:T(8,128)} fusion(f32[32,16,128,128]{3,2,1,0:T(8,128)} %fusion.5, f32[32,32]{1,0:T(8,128)S(1)} %copy-done), kind=kOutput, calls=%fused_computation.15 | convolution fusion | flops 3221225472 | bytes 67112960 | tf_op jit(solution)/shard_map/sopyz,co->scpyz/dot_general | solution.py:167
  992.9 29.0 %all-to-all-done.3 = f32[1,32,128,2,128]{4,3,1,0,2:T(2,128)} async-done(((f32[1,32,128,2,128]{4,3,1,0,2:T(2,128)}), f32[1,32,128,2,128]{4,3,1,0,2:T(2,128)}, u32[]{:S(2)}, u32[]{:S(2)}) %all-to-all-start.3) | async-done | bytes 4194336 | tf_op jit(solution)/shard_map/all_to_all | solution.py:163
  1028.5 10.9 reshape.393
  1039.4 11.2 fusion.110
  1050.6 9.0 copy.193
  1059.7 9.1 copy.192
  1068.8 8.6 bitcast_negate_fusion
  1077.4 18.5 %maximum_bitcast_fusion.16 = (f32[1,32,16,1,64,32]{4,5,3,2,1,0:T(8,128)}, f32[1,32,16,1,64,32]{4,5,3,2,1,0:T(8,128)}) fusion(f32[1,32,16,32,32]{3,4,2,1,0:T(8,128)} %bitcast_negate_fusion, f32[1,32,16,32,32]{3,4,2,1,0:T(8,128)} %bitcast.332, f32[1,32,16,32,32]{3,4,2,1,0:T(8,128)} %bitcast.328), kind=kLoop, calls=%fused_computation.94 | loop fusion | flops 2097152 | bytes 14680064 | tf_op jit(solution)/shard_map/stack | solution.py:66
  1095.9 17.3 %fusion.52 = f32[1,32,16,2,128,32]{4,5,3,2,1,0:T(8,128)S(1)} fusion(f32[1,32,16,1,64,32]{4,5,3,2,1,0:T(8,128)} %get-tuple-element.29, f32[1,32,16,1,64,32]{4,5,3,2,1,0:T(8,128)} %get-tuple-element.28, f32[128,32]{0,1:T(8,128)S(1)} %get-tuple-element.47, f32[128,32]{0,1:T(8,128)S(1)} %get-tuple-element.46), kind=kOutput, calls=%fused_computation.78 | convolution fusion | flops 3223330816 | bytes 25198592 | tf_op jit(solution)/shard_map/scpwjk,yj->scpwyk/dot_general | solution.py:73
  1120.1 61.6 %fusion.9 = f32[1,32,16,128,128]{4,3,2,1,0:T(8,128)} fusion(f32[16,128,128,32]{2,3,1,0:T(8,128)} %fusion.10, f32[1,32,16,128,32]{3,4,2,1,0:T(8,128)} %get-tuple-element.17, f32[1,32,16,128,32]{3,4,2,1,0:T(8,128)} %get-tuple-element.16, f32[128,32]{0,1:T(8,128)S(1)} %copy-done.7, f32[128,32]{0,1:T(8,128)S(1)} %copy-done.10), kind=kOutput, calls=%fused_computation.14 | convolution fusion | flops 6455042048 | bytes 83918848 | tf_op jit(solution)/shard_map/scpyj,zj->scpyz/dot_general | solution.py:75
  (64 shorter events, 64.4 us)
Async XLA Ops:
  7.2 290.8 %copy-start = (f32[32,32]{1,0:T(8,128)S(1)}, f32[32,32]{1,0:T(8,128)}, u32[]{:S(2)}) copy-start(f32[32,32]{1,0:T(8,128)} %param.8) | copy-start | bytes 12292
  7.2 263.7 %all-gather.2.cloned.1.call-start = ((), (), s32[]{:S(2)}) async-start(), calls=%async_computation.5 | async-start | bytes 41943040 | tf_op jit(solution)/shard_map/all_gather | solution.py:140
  8.0 25.5 %copy-start.5 = (f32[128,32]{0,1:T(8,128)}, f32[128,32]{0,1:T(8,128)S(1)}, u32[]{:S(2)}) copy-start(f32[128,32]{0,1:T(8,128)S(1)} %get-tuple-element.48) | copy-start | bytes 49156
  8.0 25.5 %copy-start.8 = (f32[128,32]{0,1:T(8,128)}, f32[128,32]{0,1:T(8,128)S(1)}, u32[]{:S(2)}) copy-start(f32[128,32]{0,1:T(8,128)S(1)} %get-tuple-element.49) | copy-start | bytes 49156
  124.5 101.1 %all-to-all-start = ((f32[8,1,131072]{2,1,0:T(1,128)}), f32[8,1,131072]{2,1,0:T(1,128)}, u32[]{:S(2)}, u32[]{:S(2)}) async-start(f32[8,1,131072]{2,1,0:T(1,128)} %reshape.417), calls=%async_computation | async-start | bytes 8388608 | tf_op jit(solution)/shard_map/all_to_all | solution.py:136
  132.3 151.7 %copy-start.11 = (f32[128]{0:T(128)}, f32[128]{0:T(128)S(1)}, u32[]{:S(2)}) copy-start(f32[128]{0:T(128)S(1)} %fusion.97) | copy-start | bytes 1540
  270.9 13.0 %copy-start.1 = (f32[32,128,32]{1,0,2:T(8,128)}, f32[32,128,32]{1,0,2:T(8,128)S(1)}, u32[]{:S(2)}) copy-start(f32[32,128,32]{1,0,2:T(8,128)S(1)} %get-tuple-element.36) | copy-start | bytes 1572868
  270.9 13.0 %copy-start.3 = (f32[32,128,32]{1,0,2:T(8,128)}, f32[32,128,32]{1,0,2:T(8,128)S(1)}, u32[]{:S(2)}) copy-start(f32[32,128,32]{1,0,2:T(8,128)S(1)} %get-tuple-element.37) | copy-start | bytes 1572868
  293.4 97.1 %all-to-all-start.1 = ((f32[1,32,128,2,128]{4,3,1,0,2:T(2,128)}), f32[1,32,128,2,128]{4,3,1,0,2:T(2,128)}, u32[]{:S(2)}, u32[]{:S(2)}) async-start(f32[1,32,128,2,128]{4,3,1,0,2:T(2,128)} %copy.99), calls=%async_computation.1 | async-start | bytes 8388608 | tf_op jit(solution)/shard_map/all_to_all | solution.py:144
  297.9 883.8 %reduce-scatter.2.cloned.1.call-start = ((), (), s32[]{:S(2)}) async-start(), calls=%async_computation.6 | async-start | bytes 41943040 | tf_op jit(solution)/shard_map/reduce_scatter | solution.py:159
  478.9 7.0 copy-start.6
  478.9 7.0 copy-start.9
  485.9 59.0 %copy-start.13 = (f32[32]{0:T(128)S(1)}, f32[32]{0:T(128)}, u32[]{:S(2)}) copy-start(f32[32]{0:T(128)} %param.9) | copy-start | bytes 388
  863.6 17.5 %copy-start.12 = (f32[128]{0:T(128)S(1)}, f32[128]{0:T(128)}, u32[]{:S(2)}) copy-start(f32[128]{0:T(128)} %copy-done.11) | copy-start | bytes 1540
  863.6 17.6 %copy-start.2 = (f32[32,128,32]{1,0,2:T(8,128)S(1)}, f32[32,128,32]{1,0,2:T(8,128)}, u32[]{:S(2)}) copy-start(f32[32,128,32]{1,0,2:T(8,128)} %copy-done.1) | copy-start | bytes 1572868
  863.6 17.6 %copy-start.4 = (f32[32,128,32]{1,0,2:T(8,128)S(1)}, f32[32,128,32]{1,0,2:T(8,128)}, u32[]{:S(2)}) copy-start(f32[32,128,32]{1,0,2:T(8,128)} %copy-done.3) | copy-start | bytes 1572868
  926.4 95.5 %all-to-all-start.3 = ((f32[1,32,128,2,128]{4,3,1,0,2:T(2,128)}), f32[1,32,128,2,128]{4,3,1,0,2:T(2,128)}, u32[]{:S(2)}, u32[]{:S(2)}) async-start(f32[1,32,128,2,128]{4,3,1,0,2:T(2,128)} %copy.113), calls=%async_computation.3 | async-start | bytes 8388608 | tf_op jit(solution)/shard_map/all_to_all | solution.py:163
  1113.2 6.9 copy-start.7
  1113.2 6.9 copy-start.10
Sparse Core Ops, SparseCore 0:
  9.6 208.7 all-gather.1
  898.8 233.7 reduce-scatter.1
where the time goes:
time: 1200 us; the launch traced here: 1190 us
  matrix products  371 us (31%)
  other arithmetic  302 us (25%)
  local copies, waits for them, and re-layouts  227 us (19%)
  waiting for transfers between devices  159 us (13%)
  blocking collectives  97.7 us (8%)
  starting transfers between devices  17.1 us (1%)
  between operations  14.7 us (1%)
    dot_general x2, matrix products, inverse_plane(): return jnp.einsum('scpyj,zj->scpyz', merged, table_z, precision=HIGHEST)  121 us
    all_to_all x1, blocking collectives, shards(): lax.all_to_all(forward_plane(grad_pre, table_y, table_z), 'mp', split_axi...  97.7 us
    all_to_all x1, waiting for transfers between devices, shards(): lax.all_to_all(forward_plane(fields, table_y, table_z), 'mp', split_axis=...  93.2 us
    unnamed x37, local copies, waits for them, and re-layouts  89.1 us
    another operation x1, other arithmetic  87.5 us
    dot_general x1, matrix products, shards(): jnp.einsum('sopyz,co->scpyz', grad_pre, point_weight, precision=HIGHEST)  61.9 us
    dot_general x1, matrix products, shards(): jnp.einsum('scpyz,co->sopyz', fields, point_weight, precision=HIGHEST)  56.8 us
    dot_general x2, matrix products, forward_plane(): jnp.einsum('scpyz,yj->scpjz', grid_field, table_y, precision=HIGHEST)  50.6 us
  transfers between devices with their start and end apart: 5, of which 3 were waited for; matrix products, arithmetic and copies ran while one was open for 39% of the time, Pallas kernels for 0%

commit v1 on v0

v1 whole, which is shorter than its diff:
```python
from functools import partial
import math

import jax
import jax.numpy as jnp
import ml_dtypes
import numpy as np
from jax import lax
from jax.experimental import pallas as pl
from jax.experimental.pallas import tpu as pltpu
from jax.sharding import PartitionSpec as P

NX = 128
NY = 128
NZ = 128
MX = 32
MY = 32
MZ = 32
CELLS = NX * NY * NZ
HI = 8
LO = MY // HI
LANES = LO * MZ
CHUNKS = 2
PARTS = 4
F32 = jnp.float32
BF16 = jnp.bfloat16
VMEM_BYTES = 56 * 1024 * 1024


def signed(j, kept):
    return np.where(j < kept // 2, j, j - kept)


def second_order(slabs, half):
    parts = slabs // HI
    each = LO // parts
    at = np.arange(MY).reshape(HI, LO)
    place = (at // LO) * parts + (at % LO) // each
    slab = ((place % 2) ^ half) * (slabs // 2) + place // 2
    return slab * each + at % each


def waves(number, frequencies):
    phases = np.mod(np.arange(number)[:, None] * frequencies[None, :], number) * (2.0 * np.pi / number)
    return np.cos(phases), np.sin(phases)


def two_parts(table):
    high = table.astype(ml_dtypes.bfloat16)
    low = (table - high.astype(np.float64)).astype(ml_dtypes.bfloat16)
    return high, low


def stack_left(table):
    high, low = two_parts(table)
    return np.concatenate([high, high, low], axis=1)


def stack_right(table):
    high, low = two_parts(table)
    return np.concatenate([high, high, low], axis=0)


def y_forward(slabs, half):
    cos, sin = waves(NY, signed(np.arange(MY), MY))
    order = second_order(slabs, half)
    rows = np.stack([cos[:, order], sin[:, order]], axis=0)
    table = rows.transpose(3, 0, 2, 1).reshape(LO * 2 * HI, NY)
    high, low = two_parts(table)
    top = np.concatenate([high, high], axis=1)
    bottom = np.concatenate([low, np.zeros_like(low)], axis=1)
    return np.concatenate([top, bottom], axis=0)


def y_inverse(slabs, half):
    cos, sin = waves(NY, signed(np.arange(MY), MY))
    order = second_order(slabs, half)
    rows = np.stack([cos[:, order], -sin[:, order]], axis=0)
    return stack_left(rows.transpose(1, 3, 0, 2).reshape(NY, LO * 2 * HI))


def mode_factor():
    return np.where(np.arange(MZ) == 0, 1.0, 2.0) / CELLS


def z_forward(scaled):
    cos, sin = waves(NZ, np.arange(MZ))
    scale = mode_factor() if scaled else np.ones(MZ)
    small = np.zeros((2, NZ, 2, MZ))
    small[0, :, 0] = cos * scale
    small[1, :, 0] = -sin * scale
    small[0, :, 1] = -sin * scale
    small[1, :, 1] = -cos * scale
    table = np.zeros((LO, 2, NZ, 2, LO, MZ))
    for a in range(LO):
        table[a, :, :, :, a, :] = small
    return stack_right(table.reshape(LO * 2 * NZ, 2 * LANES))


def z_inverse(scaled):
    cos, sin = waves(NZ, np.arange(MZ))
    scale = mode_factor() if scaled else np.ones(MZ)
    small = np.zeros((2, MZ, 2, NZ))
    small[0, :, 0] = (cos * scale).T
    small[1, :, 0] = (-sin * scale).T
    small[0, :, 1] = (sin * scale).T
    small[1, :, 1] = (cos * scale).T
    table = np.zeros((2, LO, MZ, LO, 2, NZ))
    for a in range(LO):
        table[:, a, :, a, :, :] = small
    return stack_right(table.reshape(2 * LANES, LO * 2 * NZ))


def x_table(groups, slabs, half, group):
    cos, sin = waves(NX, signed(np.arange(MX), MX))
    near = slabs // 2
    cells = NX // slabs
    order = np.arange(MX).reshape(groups, MX // groups)[np.arange(groups) ^ group]
    rows = slice(half * (NX // 2), (half + 1) * (NX // 2))
    return [t[rows][:, order].reshape(near, cells, groups, MX // groups) for t in (cos, sin)]


def x_forward(groups, slabs, half, group):
    cos, sin = [t.transpose(2, 3, 0, 1) for t in x_table(groups, slabs, half, group)]
    table = np.zeros((groups, 2, MX // groups, slabs // 2, 2, NX // slabs))
    table[:, 0, :, :, 0] = cos
    table[:, 0, :, :, 1] = sin
    table[:, 1, :, :, 0] = -sin
    table[:, 1, :, :, 1] = cos
    return stack_left(table.reshape(2 * MX, NX))


def x_inverse(groups, slabs, half, group):
    cos, sin = [t.transpose(0, 1, 2, 3) for t in x_table(groups, slabs, half, group)]
    table = np.zeros((slabs // 2, 2, NX // slabs, groups, 2, MX // groups))
    table[:, 0, :, :, 0] = cos
    table[:, 0, :, :, 1] = -sin
    table[:, 1, :, :, 0] = sin
    table[:, 1, :, :, 1] = cos
    return stack_left(table.reshape(NX, 2 * MX))


def split(values):
    high = values.astype(BF16)
    return high, (values - high.astype(F32)).astype(BF16)


def dot(left, right):
    return jnp.dot(left, right, preferred_element_type=F32)


def rows3(values):
    high, low = split(values)
    return jnp.concatenate([high, low, high], axis=0)


def lanes3(values):
    high, low = split(values)
    return jnp.concatenate([high, low, high], axis=1)


def y_step(planes, table_y):
    high, low = split(planes)
    products = dot(table_y, jnp.concatenate([high, low], axis=0))
    half = products.shape[0] // 2
    sums = products[:half] + products[half:]
    count = planes.shape[1] // NZ
    return jnp.concatenate(
        [
            jnp.concatenate(
                [sums[HI * k : HI * (k + 1), NZ * n : NZ * (n + 1)] for n in range(count)], axis=0
            )
            for k in range(2 * LO)
        ],
        axis=1,
    )


def y_step_back(rows, table_y):
    count = rows.shape[0] // HI
    stacked = jnp.concatenate(
        [
            jnp.concatenate(
                [rows[HI * n : HI * (n + 1), NZ * k : NZ * (k + 1)] for n in range(count)], axis=1
            )
            for k in range(2 * LO)
        ],
        axis=0,
    )
    return dot(table_y, rows3(stacked))


def put_modes(out_ref, products, channels, cells):
    for c in range(channels):
        rows = products[c * cells * HI : (c + 1) * cells * HI]
        for part in range(2):
            piece = rows[:, part * LANES : (part + 1) * LANES].reshape(cells, HI, LANES)
            out_ref[:, c, part * cells : (part + 1) * cells, :] = jnp.swapaxes(piece, 0, 1)


def take_modes(modes_ref, channels, cells):
    pieces = []
    for c in range(channels):
        parts = [
            jnp.swapaxes(modes_ref[:, c, part * cells : (part + 1) * cells, :], 0, 1).reshape(
                cells * HI, LANES
            )
            for part in range(2)
        ]
        pieces.append(jnp.concatenate(parts, axis=1))
    return jnp.concatenate(pieces, axis=0)


def channel_rows(c, cells):
    return pl.ds(pl.multiple_of(c * cells * HI, cells * HI), cells * HI)


def forward_kernel(channels, cells, field_ref, ty_ref, tz_ref, out_ref, left_ref):
    def body(c, carry):
        planes = jnp.concatenate([field_ref[0, c, x] for x in range(cells)], axis=1)
        left_ref[channel_rows(c, cells), :] = lanes3(y_step(planes, ty_ref[...]))
        return carry

    lax.fori_loop(0, channels, body, 0, unroll=2)
    put_modes(out_ref, dot(left_ref[...], tz_ref[...]), channels, cells)


def gelu_slope(x):
    return 0.5 * (1.0 + lax.erf(x * math.sqrt(0.5))) + x * (
        jnp.exp(-0.5 * x * x) * (1.0 / math.sqrt(2.0 * math.pi))
    )


def middle_kernel(
    channels, cells, modes_ref, point_ref, up_ref, tzi_ref, tyi_ref, ty_ref, tz_ref,
    grad_ref, out_ref, line_ref, left_ref,
):
    line_ref[...] = dot(lanes3(take_modes(modes_ref, channels, cells)), tzi_ref[...])

    def body(c, carry):
        rows = channel_rows(c, cells)
        spectral = y_step_back(line_ref[rows, :], tyi_ref[...])
        grads = []
        for x in range(cells):
            slope = gelu_slope(spectral[:, NZ * x : NZ * (x + 1)] + point_ref[0, c, x])
            grads.append(up_ref[0, c, x].astype(F32) * slope)
            grad_ref[0, c, x] = grads[x]
        left_ref[rows, :] = lanes3(y_step(jnp.concatenate(grads, axis=1), ty_ref[...]))
        return carry

    lax.fori_loop(0, channels, body, 0)
    put_modes(out_ref, dot(left_ref[...], tz_ref[...]), channels, cells)


def final_kernel(channels, cells, modes_ref, point_ref, tzi_ref, tyi_ref, out_ref, line_ref):
    line_ref[...] = dot(lanes3(take_modes(modes_ref, channels, cells)), tzi_ref[...])

    def body(c, carry):
        spectral = y_step_back(line_ref[channel_rows(c, cells), :], tyi_ref[...])
        for x in range(cells):
            out_ref[0, c, x] = spectral[:, NZ * x : NZ * (x + 1)] + point_ref[0, c, x]
        return carry

    lax.fori_loop(0, channels, body, 0, unroll=2)


def point_kernel(rows, field_ref, map_ref, bias_ref, *refs):
    out_ref = refs[-1]
    maps = map_ref[...]
    bias = bias_ref[...]
    channels = field_ref.shape[1]
    for r in range(0, rows, 16):
        pair = jnp.concatenate(
            [
                field_ref[0, :, 0, r : r + 8, :].reshape(channels * 8, NZ),
                field_ref[0, :, 0, r + 8 : r + 16, :].reshape(channels * 8, NZ),
            ],
            axis=1,
        )
        result = dot(maps, rows3(pair))
        out_ref[0, :, 0, r : r + 8, :] = (result[:, :NZ] + bias).reshape(channels, 8, NZ)
        out_ref[0, :, 0, r + 8 : r + 16, :] = (result[:, NZ:] + bias).reshape(channels, 8, NZ)


def whole(array):
    return pl.BlockSpec(array.shape, lambda *i: (0,) * array.ndim)


class Order:
    def __init__(self):
        self.token = None

    def call(self, kernel, operands, *, grid, in_specs, out_specs, out_shape, name, scratch=(), aliases=None, deps=()):
        many = isinstance(out_shape, (list, tuple))
        shapes = list(out_shape) if many else [out_shape]
        specs = list(out_specs) if many else [out_specs]
        count, outs = len(operands), len(shapes)
        first = self.token is None
        extra = ([] if first else [self.token]) + list(deps)
        anywhere = pl.BlockSpec(memory_space=pl.ANY)

        def body(*refs):
            given = count + len(extra)
            kernel(*refs[:count], *refs[given : given + outs], *refs[given + outs + 1 :])

        results = pl.pallas_call(
            body,
            grid=grid,
            in_specs=list(in_specs) + [anywhere] * len(extra),
            out_specs=specs + [anywhere],
            out_shape=shapes + [jax.ShapeDtypeStruct((8, 128), F32)],
            scratch_shapes=list(scratch),
            input_output_aliases=aliases or {},
            compiler_params=pltpu.CompilerParams(
                dimension_semantics=("arbitrary",) * len(grid), vmem_limit_bytes=VMEM_BYTES
            ),
            name=name,
        )(*operands, *extra)
        self.token = results[-1]
        return results[:-1] if many else results[0]


def forward_planes(order, fields, q, ty, tz):
    cells = fields.shape[2]
    per_chunk = fields.shape[1] // CHUNKS
    step = min(4, per_chunk)
    return order.call(
        partial(forward_kernel, step, cells),
        [fields, ty, tz],
        grid=(per_chunk // step,),
        in_specs=[
            pl.BlockSpec((1, step, cells, NY, NZ), lambda i: (0, q * (per_chunk // step) + i, 0, 0, 0)),
            whole(ty),
            whole(tz),
        ],
        out_specs=pl.BlockSpec((HI, step, 2 * cells, LANES), lambda i: (0, i, 0, 0)),
        out_shape=jax.ShapeDtypeStruct((HI, per_chunk, 2 * cells, LANES), F32),
        scratch=[pltpu.VMEM((step * cells * HI, 3 * 2 * LO * NZ), BF16)],
        name="planes_to_modes",
    )


def middle_planes(order, modes, point, upstream, q, tzi, tyi, ty, tz):
    cells = point.shape[2]
    per_chunk = point.shape[1] // CHUNKS
    step = min(4, per_chunk)
    modes_spec = pl.BlockSpec((HI, step, 2 * cells, LANES), lambda i: (0, i, 0, 0))
    cells_spec = pl.BlockSpec(
        (1, step, cells, NY, NZ), lambda i: (0, q * (per_chunk // step) + i, 0, 0, 0)
    )
    return order.call(
        partial(middle_kernel, step, cells),
        [modes, point, upstream, tzi, tyi, ty, tz],
        grid=(per_chunk // step,),
        in_specs=[modes_spec, cells_spec, cells_spec, whole(tzi), whole(tyi), whole(ty), whole(tz)],
        out_specs=[cells_spec, modes_spec],
        out_shape=[
            jax.ShapeDtypeStruct(point.shape, F32),
            jax.ShapeDtypeStruct((HI, per_chunk, 2 * cells, LANES), F32),
        ],
        scratch=[
            pltpu.VMEM((step * cells * HI, 2 * LO * NZ), F32),
            pltpu.VMEM((step * cells * HI, 3 * 2 * LO * NZ), BF16),
        ],
        aliases={1: 0},
        name="modes_to_gradient_to_modes",
    )


def final_planes(order, modes, point, q, tzi, tyi):
    cells = point.shape[2]
    per_chunk = point.shape[1] // CHUNKS
    step = min(4, per_chunk)
    cells_spec = pl.BlockSpec(
        (1, step, cells, NY, NZ), lambda i: (0, q * (per_chunk // step) + i, 0, 0, 0)
    )
    return order.call(
        partial(final_kernel, step, cells),
        [modes, point, tzi, tyi],
        grid=(per_chunk // step,),
        in_specs=[
            pl.BlockSpec((HI, step, 2 * cells, LANES), lambda i: (0, i, 0, 0)),
            cells_spec,
            whole(tzi),
            whole(tyi),
        ],
        out_specs=cells_spec,
        out_shape=jax.ShapeDtypeStruct(point.shape, F32),
        scratch=[pltpu.VMEM((step * cells * HI, 2 * LO * NZ), F32)],
        aliases={1: 0},
        name="modes_to_planes",
    )


def point_table_kernel(weight_ref, spread_ref, out_ref):
    spread = spread_ref[...]
    size = spread.shape[0]
    row = lax.broadcasted_iota(jnp.int32, (size, size), 0)
    column = lax.broadcasted_iota(jnp.int32, (size, size), 1)
    same = jnp.bitwise_and(row, 7) == jnp.bitwise_and(column, 7)
    parts = []
    for part in split(weight_ref[...]):
        left = dot(spread, part).astype(BF16)
        full = lax.dot_general(left, spread, (((1,), (1,)), ((), ())), preferred_element_type=F32)
        parts.append(jnp.where(same, full, 0.0).astype(BF16))
    out_ref[...] = jnp.concatenate([parts[0], parts[0], parts[1]], axis=1)


def point_tables(weight, bias):
    channels = bias.shape[0]
    spread = np.repeat(np.eye(channels), 8, axis=0).astype(ml_dtypes.bfloat16)
    mapping = pl.pallas_call(
        point_table_kernel,
        out_shape=jax.ShapeDtypeStruct((channels * 8, channels * 8 * 3), BF16),
        name="channel_table",
    )(weight.T, jnp.asarray(spread))
    return mapping, jnp.broadcast_to(jnp.repeat(bias, 8)[:, None], (channels * 8, NZ))


def point_map(order, fields, tables, q, buffer, deps=()):
    channels, cells = fields.shape[1], fields.shape[2]
    rows = NY
    part = cells // PARTS
    mapping, shift = tables
    spec = pl.BlockSpec((1, channels, 1, rows, NZ), lambda i, j: (0, 0, q * part + i, j, 0))
    operands = [fields, mapping, shift]
    specs = [spec, whole(mapping), whole(shift)]
    aliases = {}
    if buffer is not None:
        operands.append(buffer)
        specs.append(pl.BlockSpec(memory_space=pl.ANY))
        aliases = {3: 0}
    return order.call(
        partial(point_kernel, rows),
        [*operands],
        grid=(part, NY // rows),
        in_specs=specs,
        out_specs=spec,
        out_shape=jax.ShapeDtypeStruct(fields.shape, F32),
        aliases=aliases,
        deps=deps,
        name="channel_map",
    )


def channel_pairs(refs, channels):
    for c in range(0, channels, 2):
        yield c, jnp.concatenate(
            [
                jnp.concatenate([ref[:, c + k].reshape(-1, ref.shape[-1]) for ref in refs], axis=0)
                for k in range(2)
            ],
            axis=1,
        )


def line_send_kernel(data_ref, table_ref, out_ref):
    lanes = data_ref.shape[-1]
    for c, pair in channel_pairs([data_ref.at[:, 0]], data_ref.shape[2]):
        result = dot(table_ref[...], rows3(pair))
        for k in range(2):
            out_ref[c + k] = result[:, k * lanes : (k + 1) * lanes]


def line_keep_kernel(data_ref, other_ref, table_ref, *out_refs):
    lanes = data_ref.shape[-1]
    rows = out_refs[0].shape[1]
    for c, pair in channel_pairs([data_ref.at[:, 0]], data_ref.shape[2]):
        result = dot(table_ref[...], rows3(pair))
        for k in range(2):
            total = result[:, k * lanes : (k + 1) * lanes] + other_ref[c + k]
            for g, out_ref in enumerate(out_refs):
                out_ref[c + k] = total[g * rows : (g + 1) * rows]


def line_send(order, data, table):
    near, _, channels, rows, lanes = data.shape
    modes = table.shape[0]
    step = min(8, channels)
    return order.call(
        line_send_kernel,
        [data, table],
        grid=(channels // step,),
        in_specs=[
            pl.BlockSpec((near, 1, step, rows, lanes), lambda i: (0, 1, i, 0, 0)),
            whole(table),
        ],
        out_specs=pl.BlockSpec((step, modes, lanes), lambda i: (i, 0, 0)),
        out_shape=jax.ShapeDtypeStruct((channels, modes, lanes), F32),
        name="partner_modes",
    )


def line_keep(order, data, other, table, groups):
    near, _, channels, rows, lanes = data.shape
    modes = table.shape[0]
    step = min(8, channels)
    return order.call(
        line_keep_kernel,
        [data, other, table],
        grid=(channels // step,),
        in_specs=[
            pl.BlockSpec((near, 1, step, rows, lanes), lambda i: (0, 0, i, 0, 0)),
            pl.BlockSpec((step, modes, lanes), lambda i: (i, 0, 0)),
            whole(table),
        ],
        out_specs=[pl.BlockSpec((step, modes // groups, lanes), lambda i: (i, 0, 0))] * groups,
        out_shape=[jax.ShapeDtypeStruct((channels, modes // groups, lanes), F32)] * groups,
        name="own_modes",
    )


def line_back_kernel(own_ref, other_ref, table_ref, out_ref):
    lanes = own_ref.shape[-1]
    near, _, channels, rows, _ = out_ref.shape
    for part, ref in enumerate((own_ref, other_ref)):
        for c, pair in channel_pairs([ref], channels):
            result = dot(table_ref[...], rows3(pair))
            for k in range(2):
                out_ref[:, part, c + k] = result[:, k * lanes : (k + 1) * lanes].reshape(
                    near, rows, lanes
                )


def line_back(order, own, other, table, near, deps=()):
    groups, channels, rows, lanes = own.shape
    step = min(8, channels)
    rows_out = table.shape[0] // near
    return order.call(
        line_back_kernel,
        [own, other, table],
        grid=(channels // step,),
        in_specs=[pl.BlockSpec((groups, step, rows, lanes), lambda i: (0, i, 0, 0))] * 2
        + [whole(table)],
        out_specs=pl.BlockSpec((near, 2, step, rows_out, lanes), lambda i: (0, 0, i, 0, 0)),
        out_shape=jax.ShapeDtypeStruct((near, 2, channels, rows_out, lanes), F32),
        deps=deps,
        name="modes_to_cells",
    )


def mix_kernel(adjoint, groups, *refs):
    spec_refs, weight_ref, out_refs = refs[: CHUNKS * groups], refs[CHUNKS * groups], refs[-groups:]
    per_chunk = spec_refs[0].shape[0]
    rows = out_refs[0].shape[1] // 2
    for o in range(out_refs[0].shape[0]):
        real = [None] * groups
        imag = [None] * groups
        for i in range(CHUNKS * per_chunk):
            at = (o, i) if adjoint else (i, o)
            wr, wi = weight_ref[0, at[0], at[1]], weight_ref[1, at[0], at[1]]
            for s in range(groups):
                spec_ref = spec_refs[(i // per_chunk) * groups + s]
                sr = spec_ref[i % per_chunk, :rows]
                si = spec_ref[i % per_chunk, rows:]
                if adjoint:
                    re, im = wr * sr + wi * si, wr * si - wi * sr
                else:
                    re, im = wr * sr - wi * si, wr * si + wi * sr
                real[s] = re if i == 0 else real[s] + re
                imag[s] = im if i == 0 else imag[s] + im
        for s in range(groups):
            out_refs[s][o, :rows] = real[s]
            out_refs[s][o, rows:] = imag[s]


def mix(order, spectra, weight, q, adjoint):
    groups = len(spectra[0])
    per_chunk, rows, lanes = spectra[0][0].shape
    channels = weight.shape[1]
    step = 4
    if adjoint:
        block = (2, step, channels, rows // 2, lanes)
        place = lambda i: (0, q * (per_chunk // step) + i, 0, 0, 0)
    else:
        block = (2, channels, step, rows // 2, lanes)
        place = lambda i: (0, 0, q * (per_chunk // step) + i, 0, 0)
    flat = [piece for chunk in spectra for piece in chunk]
    return order.call(
        partial(mix_kernel, adjoint, groups),
        [*flat, weight],
        grid=(per_chunk // step,),
        in_specs=[whole(s) for s in flat] + [pl.BlockSpec(block, place)],
        out_specs=[pl.BlockSpec((step, rows, lanes), lambda i: (i, 0, 0))] * groups,
        out_shape=[jax.ShapeDtypeStruct((per_chunk, rows, lanes), F32)] * groups,
        name="mix_back" if adjoint else "mix",
    )


def weight_kernel(groups, *refs):
    grad_refs, spec_refs, out_ref = refs[: CHUNKS * groups], refs[CHUNKS * groups : -1], refs[-1]
    per_chunk = grad_refs[0].shape[0]
    rows = grad_refs[0].shape[1] // 2
    for i in range(out_ref.shape[1]):
        sr = [spec_refs[s][i, :rows] for s in range(groups)]
        si = [spec_refs[s][i, rows:] for s in range(groups)]
        for o in range(out_ref.shape[2]):
            real = imag = None
            for s in range(groups):
                grad_ref = grad_refs[(o // per_chunk) * groups + s]
                gr = grad_ref[o % per_chunk, :rows]
                gi = grad_ref[o % per_chunk, rows:]
                re, im = gr * sr[s] + gi * si[s], gi * sr[s] - gr * si[s]
                real = re if s == 0 else real + re
                imag = im if s == 0 else imag + im
            out_ref[0, i, o] = real
            out_ref[1, i, o] = imag


def weight_gradient(order, gradients, spectra, q, buffer, deps=()):
    groups = len(spectra)
    per_chunk, rows, lanes = spectra[0].shape
    channels = per_chunk * CHUNKS
    step = 2
    flat = [piece for chunk in gradients for piece in chunk]
    operands = flat + list(spectra)
    specs = [whole(g) for g in flat] + [
        pl.BlockSpec((step, rows, lanes), lambda i: (i, 0, 0)) for _ in spectra
    ]
    aliases = {}
    kernel = partial(weight_kernel, groups)
    if buffer is not None:
        aliases = {len(operands): 0}
        operands = operands + [buffer]
        specs = specs + [pl.BlockSpec(memory_space=pl.ANY)]
        kernel = lambda *refs: weight_kernel(groups, *refs[:-2], refs[-1])
    return order.call(
        kernel,
        [*operands],
        grid=(per_chunk // step,),
        in_specs=specs,
        out_specs=pl.BlockSpec(
            (2, step, channels, rows // 2, lanes),
            lambda i: (0, q * (per_chunk // step) + i, 0, 0, 0),
        ),
        out_shape=jax.ShapeDtypeStruct((2, channels, channels, rows // 2, lanes), F32),
        aliases=aliases,
        deps=deps,
        name="weight_gradient",
    )


def cut_lanes(modes, slabs):
    parts = slabs // HI
    if parts == 1:
        return modes
    _, channels, rows, lanes = modes.shape
    cut = modes.reshape(HI, channels, rows, parts, lanes // parts)
    return cut.transpose(0, 3, 1, 2, 4).reshape(slabs, channels, rows, lanes // parts)


def join_lanes(modes, slabs):
    parts = slabs // HI
    if parts == 1:
        return modes
    _, channels, rows, lanes = modes.shape
    cut = modes.reshape(HI, parts, channels, rows, lanes)
    return cut.transpose(0, 2, 3, 1, 4).reshape(HI, channels, rows, lanes * parts)


def shards(groups, slabs, fields, upstream, spectral_weight, point_weight, point_bias):
    near = slabs // 2
    half = lax.axis_index("mp") // near
    group = lax.axis_index("dp")

    def pick(tables, index):
        return lax.dynamic_index_in_dim(jnp.asarray(np.stack(tables)), index, 0, False)

    both = [(h, g) for h in range(2) for g in range(groups)]
    tx = pick([x_forward(groups, slabs, h, g) for h, g in both], half * groups + group)
    txi = pick([x_inverse(groups, slabs, h, g) for h, g in both], half * groups + group)
    ty = pick([y_forward(slabs, h) for h in range(2)], half)
    tyi = pick([y_inverse(slabs, h) for h in range(2)], half)
    tz, tz_scaled = jnp.asarray(z_forward(False)), jnp.asarray(z_forward(True))
    tzi, tzi_scaled = jnp.asarray(z_inverse(False)), jnp.asarray(z_inverse(True))
    halves = [[h * near + d for d in range(near)] for h in range(2)]
    across = [(j, j ^ near) for j in range(slabs)]

    def swap_near(data):
        return lax.all_to_all(
            data, "mp", split_axis=0, concat_axis=0, axis_index_groups=halves, tiled=True
        )

    def swap_groups(pieces):
        return [pieces[0]] + [
            lax.ppermute(pieces[k], "dp", [(j, j ^ k) for j in range(groups)])
            for k in range(1, groups)
        ]

    def near_blocks(planes):
        cut = cut_lanes(planes, slabs)
        return swap_near(cut.reshape((near, 2) + cut.shape[1:]))

    point = point_tables(point_weight, point_bias)
    point_back = point_tables(point_weight.T, jnp.zeros_like(point_bias))
    order = Order()
    state = {}

    def forward(q):
        planes = forward_planes(order, fields, q, ty, tz)
        state["near", q] = near_blocks(planes)

    def send(q):
        state["other", q] = lax.ppermute(line_send(order, state["near", q], tx), "mp", across)

    def keep(q):
        pieces = line_keep(order, state["near", q], state["other", q], tx, groups)
        state["spectrum", q] = swap_groups(pieces)

    def mixed(q, spectra, adjoint):
        own = jnp.stack(swap_groups(mix(order, spectra, spectral_weight, q, adjoint)))
        state["own", q] = own, lax.ppermute(own, "mp", across)

    def back(q, *deps):
        cells = swap_near(line_back(order, *state["own", q], txi, near, deps))
        state["planes", q] = join_lanes(cells.reshape((slabs,) + cells.shape[2:]), slabs)

    def channels(source, tables, key, q, *deps):
        state[key] = point_map(order, source, tables, q, state.get(key), deps)

    def middle(q):
        state["point"], planes = middle_planes(
            order, state["planes", q], state["point"], upstream, q, tzi_scaled, tyi, ty, tz_scaled
        )
        state["near", q] = near_blocks(planes)

    def weights(q, *deps):
        state["weights"] = weight_gradient(
            order, gradients, spectra[q], q, state.get("weights"), deps
        )

    def final(q):
        state["result"] = final_planes(order, state["planes", q], state["result"], q, tzi, tyi)

    map_fields = partial(channels, fields, point, "point")
    forward(0)
    forward(1)
    map_fields(0)
    map_fields(1)
    send(0)
    map_fields(2)
    send(1)
    keep(0)
    map_fields(3)
    keep(1)
    spectra = [state["spectrum", q] for q in range(CHUNKS)]
    mixed(0, spectra, False)
    mixed(1, spectra, False)
    back(0, state["own", 1][0])
    back(1)
    middle(0)
    middle(1)
    map_back = partial(channels, state["point"], point_back, "result")
    send(0)
    map_back(0)
    map_back(1)
    send(1)
    keep(0)
    map_back(2)
    map_back(3)
    keep(1)
    gradients = [state["spectrum", q] for q in range(CHUNKS)]
    mixed(0, gradients, True)
    mixed(1, gradients, True)
    weights(0, state["own", 0][0], state["own", 1][0])
    back(0)
    weights(1)
    back(1)
    final(0)
    final(1)
    return state["result"], state["weights"]


def solution(mesh):
    placed = (
        P("dp", None, "mp", None, None),
        P("dp", None, "mp", None, None),
        P(None, None, None, "dp", "mp"),
        P(),
        P(),
    )
    return jax.shard_map(
        partial(shards, mesh.shape["dp"], mesh.shape["mp"]),
        mesh=mesh,
        in_specs=placed,
        out_specs=(P("dp", None, "mp", None, None), P(None, None, None, "dp", "mp")),
        check_vma=False,
    )
```

time: 1200 us -> 513 us (0.43)
  matrix products: 371 us -> 0 us
  other arithmetic: 302 us -> 5.36 us
  Pallas kernels: 0 us -> 257 us
  local copies, waits for them, and re-layouts: 227 us -> 22.9 us
  blocking collectives: 97.7 us -> 0 us
  starting transfers between devices: 17.1 us -> 60.2 us
  between operations: 14.7 us -> 1 us
    dot_general x14 -> x0, matrix products: 371 us -> none  [the longest x2 121 us: inverse_plane(): return jnp.einsum('scpyj,zj->scpyz', merged, table_z, precision=HIGHEST)]
    pallas_call x0 -> x34, Pallas kernels: none -> 257 us  [the longest x32 253 us: call(): pl.pallas_call(body, grid=grid, in_specs=list(in_specs) + [anywhere] * le...]
    another operation x9 -> x4, other arithmetic: 140 us -> 5.36 us  [mixed(): jnp.stack(swap_groups(mix(order, spectra, spectral_weight, q, adjoint)))]
    ppermute x0 -> x32, waiting for transfers between devices: none -> 131 us  [the longest x4 72 us: mixed(): state['own', q] = (own, lax.ppermute(own, 'mp', across))]
    all_to_all x3 -> x8, waiting for transfers between devices: 158 us -> 31.9 us  [swap_near(): lax.all_to_all(data, 'mp', split_axis=0, concat_axis=0, axis_index_groups...]
    all_to_all x1 -> x0, blocking collectives: 97.7 us -> none  [shards(): lax.all_to_all(forward_plane(grad_pre, table_y, table_z), 'mp', split_axi...]
    unnamed x37 -> x67, local copies, waits for them, and re-layouts: 89.1 us -> 16.3 us
    another operation x4 -> x0, local copies, waits for them, and re-layouts: 43.2 us -> none  [forward_plane(): result = jnp.stack([cos_cos - sin_sin, -(sin_cos + cos_sin)], axis=3)]
  transfers between devices with their start and end apart: 5 -> 40, of which waited for: 3 -> 21; matrix products, arithmetic and copies ran while one was open for 39% -> 2% of each run, Pallas kernels for 0% -> 42%
where the time goes in v1:
time: 513 us; the launch traced here: 510 us
  Pallas kernels  257 us (50%)
  waiting for transfers between devices  163 us (32%)
  starting transfers between devices  60.2 us (12%)
  local copies, waits for them, and re-layouts  22.9 us (4%)
  other arithmetic  5.36 us (1%)
    pallas_call x32, Pallas kernels, call(): pl.pallas_call(body, grid=grid, in_specs=list(in_specs) + [anywhere] * le...  253 us
    ppermute x4, waiting for transfers between devices, mixed(): state['own', q] = (own, lax.ppermute(own, 'mp', across))  72 us
    ppermute x24, waiting for transfers between devices, swap_groups(): lax.ppermute(pieces[k], 'dp', [(j, j ^ k) for j in range(groups)])  36.1 us
    all_to_all x8, starting transfers between devices, swap_near(): lax.all_to_all(data, 'mp', split_axis=0, concat_axis=0, axis_index_groups...  35.1 us
    all_to_all x8, waiting for transfers between devices, swap_near(): lax.all_to_all(data, 'mp', split_axis=0, concat_axis=0, axis_index_groups...  31.9 us
    ppermute x4, waiting for transfers between devices, send(): lax.ppermute(line_send(order, state['near', q], tx), 'mp', across)  23.1 us
    unnamed x67, local copies, waits for them, and re-layouts  16.3 us
    ppermute x24, starting transfers between devices, swap_groups(): lax.ppermute(pieces[k], 'dp', [(j, j ^ k) for j in range(groups)])  15.9 us
  transfers between devices with their start and end apart: 40, of which 21 were waited for; matrix products, arithmetic and copies ran while one was open for 2% of the time, Pallas kernels for 42%

profile of v1, /device:TPU:0, one launch (start us, length us, event | category | flops | bytes accessed | tf_op | source)
XLA Modules:
  0.0 509.8 jit_solution(1820203997411420384)
XLA Ops:
  2.1 12.3 %planes_to_modes.2 = (f32[8,16,32,128]{3,2,1,0:T(8,128)}, f32[8,128]{1,0:T(8,128)}) custom-call(f32[1,32,16,128,128]{4,3,2,1,0:T(8,128)} %refs_0_.11, bf16[128,256]{1,0:T(8,128)(2,1)} %dynamic-slice_bitcast_fusion.2.refs_1_.refs_5_, bf16[3072,256]{1,0:T(8,128)(2,1)} %constant.66.clone.refs_2_), custom_call_target="tpu_custom_call" | custom-call | tf_op jit(solution)/shard_map/planes_to_modes/pallas_call | solution.py:306
  14.4 5.2 %all-to-all-start = ((f32[4,2,16,32,128]{4,3,2,1,0:T(8,128)}), f32[4,2,16,32,128]{4,3,2,1,0:T(8,128)S(1)}, u32[]{:S(2)}, u32[]{:S(2)}) async-start(f32[4,2,16,32,128]{4,3,2,1,0:T(8,128)} %bitcast.38), calls=%async_computation | async-start | bytes 4194304 | tf_op jit(solution)/shard_map/all_to_all | solution.py:680
  19.7 12.3 %planes_to_modes.3 = (f32[8,16,32,128]{3,2,1,0:T(8,128)}, f32[8,128]{1,0:T(8,128)}) custom-call(f32[1,32,16,128,128]{4,3,2,1,0:T(8,128)} %refs_0_.11, bf16[128,256]{1,0:T(8,128)(2,1)} %dynamic-slice_bitcast_fusion.2.refs_1_.refs_5_, bf16[3072,256]{1,0:T(8,128)(2,1)} %constant.66.clone.refs_2_, f32[8,128]{1,0:T(8,128)} %get-tuple-element.92.refs_3_), custom_call_target="tpu_custom_call" | custom-call | tf_op jit(solution)/shard_map/planes_to_modes/pallas_call | solution.py:306
  32.0 12.6 %all-to-all-done.refs_0_ = f32[4,2,16,32,128]{4,3,2,1,0:T(8,128)S(1)} async-done(((f32[4,2,16,32,128]{4,3,2,1,0:T(8,128)}), f32[4,2,16,32,128]{4,3,2,1,0:T(8,128)S(1)}, u32[]{:S(2)}, u32[]{:S(2)}) %all-to-all-start) | async-done | bytes 2097184 | tf_op jit(solution)/shard_map/all_to_all | solution.py:680
  45.9 3.6 all-to-all-start.1
  53.0 9.2 %channel_map.8 = (f32[1,32,16,128,128]{4,3,2,1,0:T(8,128)}, f32[8,128]{1,0:T(8,128)}) custom-call(f32[1,32,16,128,128]{4,3,2,1,0:T(8,128)} %refs_0_.11, bf16[256,768]{1,0:T(8,128)(2,1)} %channel_table.2.refs_1_, f32[256,128]{1,0:T(8,128)} %broadcast_in_dim.15.refs_2_, f32[8,128]{1,0:T(8,128)} %get-tuple-element.93.refs_3_), custom_call_target="tpu_custom_call" | custom-call | tf_op jit(solution)/shard_map/channel_map/pallas_call | solution.py:306
  62.2 9.2 %channel_map.9 = (f32[1,32,16,128,128]{4,3,2,1,0:T(8,128)}, f32[8,128]{1,0:T(8,128)}) custom-call(f32[1,32,16,128,128]{4,3,2,1,0:T(8,128)} %refs_0_.11, bf16[256,768]{1,0:T(8,128)(2,1)} %channel_table.2.refs_1_, f32[256,128]{1,0:T(8,128)} %broadcast_in_dim.15.refs_2_, ...), custom_call_target="tpu_custom_call", output_to_operand_aliasing={{0}: (3, {})} | custom-call | tf_op jit(solution)/shard_map/channel_map/pallas_call | solution.py:306
  75.1 2.7 collective-permute-start
  77.7 9.2 %channel_map.10 = (f32[1,32,16,128,128]{4,3,2,1,0:T(8,128)}, f32[8,128]{1,0:T(8,128)}) custom-call(f32[1,32,16,128,128]{4,3,2,1,0:T(8,128)} %refs_0_.11, bf16[256,768]{1,0:T(8,128)(2,1)} %channel_table.2.refs_1_, f32[256,128]{1,0:T(8,128)} %broadcast_in_dim.15.refs_2_, ...), custom_call_target="tpu_custom_call", output_to_operand_aliasing={{0}: (3, {})} | custom-call | tf_op jit(solution)/shard_map/channel_map/pallas_call | solution.py:306
  90.8 22.7 %collective-permute-done.refs_1_ = f32[16,64,128]{2,1,0:T(8,128)S(1)} collective-permute-done((f32[16,64,128]{2,1,0:T(8,128)}, f32[16,64,128]{2,1,0:T(8,128)S(1)}, u32[]{:S(2)}, u32[]{:S(2)}) %collective-permute-start) | collective-permute-done | bytes 524320 | tf_op jit(solution)/shard_map/ppermute | solution.py:704
  114.3 2.4 own_modes.4
  118.6 9.2 %channel_map.11 = (f32[1,32,16,128,128]{4,3,2,1,0:T(8,128)}, f32[8,128]{1,0:T(8,128)}) custom-call(f32[1,32,16,128,128]{4,3,2,1,0:T(8,128)} %refs_0_.11, bf16[256,768]{1,0:T(8,128)(2,1)} %channel_table.2.refs_1_, f32[256,128]{1,0:T(8,128)} %broadcast_in_dim.15.refs_2_, ...), custom_call_target="tpu_custom_call", output_to_operand_aliasing={{0}: (3, {})} | custom-call | tf_op jit(solution)/shard_map/channel_map/pallas_call | solution.py:306
  132.9 4.9 collective-permute-done.6.refs_6_.refs_10_
  139.8 5.9 %mix.2 = (f32[16,16,128]{2,1,0:T(8,128)}, f32[16,16,128]{2,1,0:T(8,128)}, f32[16,16,128]{2,1,0:T(8,128)}, f32[16,16,128]{2,1,0:T(8,128)}, f32[8,128]{1,0:T(8,128)}) custom-call(f32[16,16,128]{2,1,0:T(8,128)} %get-tuple-element.103.refs_0_.refs_8_, f32[16,16,128]{2,1,0:T(8,128)} %copy-done.19, f32[16,16,128]{2,1,0:T(8,128)} %copy-done.20, ...), custom_call_target="tpu_custom_call" | custom-call | tf_op jit(solution)/shard_map/mix/pallas_call | solution.py:306
  147.8 5.0 collective-permute-done.9
  155.0 6.0 %mix.3 = (f32[16,16,128]{2,1,0:T(8,128)}, f32[16,16,128]{2,1,0:T(8,128)}, f32[16,16,128]{2,1,0:T(8,128)}, f32[16,16,128]{2,1,0:T(8,128)}, f32[8,128]{1,0:T(8,128)}) custom-call(f32[16,16,128]{2,1,0:T(8,128)} %get-tuple-element.103.refs_0_.refs_8_, f32[16,16,128]{2,1,0:T(8,128)} %copy-done.19, f32[16,16,128]{2,1,0:T(8,128)} %copy-done.20, ...), custom_call_target="tpu_custom_call" | custom-call | tf_op jit(solution)/shard_map/mix/pallas_call | solution.py:306
  164.8 3.5 collective-permute-done.13
  171.2 9.4 %collective-permute-done.11.refs_1_ = f32[4,16,16,128]{3,2,1,0:T(8,128)S(1)} collective-permute-done((f32[4,16,16,128]{3,2,1,0:T(8,128)S(1)}, f32[4,16,16,128]{3,2,1,0:T(8,128)S(1)}, u32[]{:S(2)}, u32[]{:S(2)}) %collective-permute-start.11) | collective-permute-done | bytes 524320 | tf_op jit(solution)/shard_map/ppermute | solution.py:712
  181.4 2.6 modes_to_cells.4
  184.0 3.7 all-to-all-start.2
  188.4 33.8 %collective-permute-done.15.refs_1_ = f32[4,16,16,128]{3,2,1,0:T(8,128)S(1)} collective-permute-done((f32[4,16,16,128]{3,2,1,0:T(8,128)S(1)}, f32[4,16,16,128]{3,2,1,0:T(8,128)S(1)}, u32[]{:S(2)}, u32[]{:S(2)}) %collective-permute-start.15) | collective-permute-done | bytes 524320 | tf_op jit(solution)/shard_map/ppermute | solution.py:712
  223.0 2.6 modes_to_cells.5
  227.0 4.7 all-to-all-start.4
  232.3 29.1 %modes_to_gradient_to_modes.2 = (f32[1,32,16,128,128]{4,3,2,1,0:T(8,128)}, f32[8,16,32,128]{3,2,1,0:T(8,128)}, f32[8,128]{1,0:T(8,128)}) custom-call(f32[8,16,32,128]{3,2,1,0:T(8,128)} %bitcast.34, f32[1,32,16,128,128]{4,3,2,1,0:T(8,128)} %get-tuple-element.127.refs_1_, bf16[1,32,16,128,128]{4,3,2,1,0:T(8,128)(2,1)} %refs_2_.7, ...), custom_call_target="tpu_custom_call", output_to_operand_aliasing={{0}: (1, {})} | custom-call | tf_op jit(solution)/shard_map/modes_to_gradient_to_modes/pallas_call | solution.py:306
  261.4 4.7 all-to-all-start.3
  266.1 29.1 %modes_to_gradient_to_modes.3 = (f32[1,32,16,128,128]{4,3,2,1,0:T(8,128)}, f32[8,16,32,128]{3,2,1,0:T(8,128)}, f32[8,128]{1,0:T(8,128)}) custom-call(f32[8,16,32,128]{3,2,1,0:T(8,128)} %bitcast.17.refs_0_, f32[1,32,16,128,128]{4,3,2,1,0:T(8,128)} %get-tuple-element.132.refs_1_, ...), custom_call_target="tpu_custom_call", output_to_operand_aliasing={{0}: (1, {})} | custom-call | tf_op jit(solution)/shard_map/modes_to_gradient_to_modes/pallas_call | solution.py:306
  296.5 4.2 all-to-all-start.5
  303.0 2.6 collective-permute-start.16
  308.2 9.2 %channel_map.12 = (f32[1,32,16,128,128]{4,3,2,1,0:T(8,128)}, f32[8,128]{1,0:T(8,128)}) custom-call(f32[1,32,16,128,128]{4,3,2,1,0:T(8,128)} %get-tuple-element.137.refs_0_, bf16[256,768]{1,0:T(8,128)(2,1)} %channel_table.3.refs_1_, f32[256,128]{1,0:T(8,128)} %broadcast_in_dim.16.refs_2_, f32[8,128]{1,0:T(8,128)} %get-tuple-element.138.refs_3_), custom_call_target="tpu_custom_call" | custom-call | tf_op jit(solution)/shard_map/channel_map/pallas_call | solution.py:306
  317.4 9.2 %channel_map.13 = (f32[1,32,16,128,128]{4,3,2,1,0:T(8,128)}, f32[8,128]{1,0:T(8,128)}) custom-call(f32[1,32,16,128,128]{4,3,2,1,0:T(8,128)} %get-tuple-element.137.refs_0_, bf16[256,768]{1,0:T(8,128)(2,1)} %channel_table.3.refs_1_, f32[256,128]{1,0:T(8,128)} %broadcast_in_dim.16.refs_2_, ...), custom_call_target="tpu_custom_call", output_to_operand_aliasing={{0}: (3, {})} | custom-call | tf_op jit(solution)/shard_map/channel_map/pallas_call | solution.py:306
  326.6 10.0 %all-to-all-done.5.refs_0_ = f32[4,2,16,32,128]{4,3,2,1,0:T(8,128)S(1)} async-done(((f32[4,2,16,32,128]{4,3,2,1,0:T(8,128)}), f32[4,2,16,32,128]{4,3,2,1,0:T(8,128)S(1)}, u32[]{:S(2)}, u32[]{:S(2)}) %all-to-all-start.5) | async-done | bytes 2097184 | tf_op jit(solution)/shard_map/all_to_all | solution.py:680
  345.3 9.2 %channel_map.14 = (f32[1,32,16,128,128]{4,3,2,1,0:T(8,128)}, f32[8,128]{1,0:T(8,128)}) custom-call(f32[1,32,16,128,128]{4,3,2,1,0:T(8,128)} %get-tuple-element.137.refs_0_, bf16[256,768]{1,0:T(8,128)(2,1)} %channel_table.3.refs_1_, f32[256,128]{1,0:T(8,128)} %broadcast_in_dim.16.refs_2_, ...), custom_call_target="tpu_custom_call", output_to_operand_aliasing={{0}: (3, {})} | custom-call | tf_op jit(solution)/shard_map/channel_map/pallas_call | solution.py:306
  354.5 9.2 %channel_map.15 = (f32[1,32,16,128,128]{4,3,2,1,0:T(8,128)}, f32[8,128]{1,0:T(8,128)}) custom-call(f32[1,32,16,128,128]{4,3,2,1,0:T(8,128)} %get-tuple-element.137.refs_0_, bf16[256,768]{1,0:T(8,128)(2,1)} %channel_table.3.refs_1_, f32[256,128]{1,0:T(8,128)} %broadcast_in_dim.16.refs_2_, ...), custom_call_target="tpu_custom_call", output_to_operand_aliasing={{0}: (3, {})} | custom-call | tf_op jit(solution)/shard_map/channel_map/pallas_call | solution.py:306
  369.1 4.7 collective-permute-done.22.refs_6_
  376.4 5.5 %mix_back.2 = (f32[16,16,128]{2,1,0:T(8,128)}, f32[16,16,128]{2,1,0:T(8,128)}, f32[16,16,128]{2,1,0:T(8,128)}, f32[16,16,128]{2,1,0:T(8,128)}, f32[8,128]{1,0:T(8,128)}) custom-call(f32[16,16,128]{2,1,0:T(8,128)} %get-tuple-element.143.refs_0_, f32[16,16,128]{2,1,0:T(8,128)} %copy-done.9, f32[16,16,128]{2,1,0:T(8,128)} %copy-done.10, ...), custom_call_target="tpu_custom_call" | custom-call | tf_op jit(solution)/shard_map/mix_back/pallas_call | solution.py:306
  383.8 4.9 collective-permute-done.29
  393.4 5.5 %mix_back.3 = (f32[16,16,128]{2,1,0:T(8,128)}, f32[16,16,128]{2,1,0:T(8,128)}, f32[16,16,128]{2,1,0:T(8,128)}, f32[16,16,128]{2,1,0:T(8,128)}, f32[8,128]{1,0:T(8,128)}) custom-call(f32[16,16,128]{2,1,0:T(8,128)} %get-tuple-element.143.refs_0_, f32[16,16,128]{2,1,0:T(8,128)} %copy-done.9, f32[16,16,128]{2,1,0:T(8,128)} %copy-done.10, ...), custom_call_target="tpu_custom_call" | custom-call | tf_op jit(solution)/shard_map/mix_back/pallas_call | solution.py:306
  400.9 5.0 collective-permute-done.25
  408.9 6.7 %weight_gradient.2 = (f32[2,32,32,8,128]{4,3,2,1,0:T(8,128)}, f32[8,128]{1,0:T(8,128)}) custom-call(f32[16,16,128]{2,1,0:T(8,128)} %get-tuple-element.143.refs_0_, f32[16,16,128]{2,1,0:T(8,128)} %copy-done.9, f32[16,16,128]{2,1,0:T(8,128)} %copy-done.10, f32[16,16,128]{2,1,0:T(8,128)} %copy-done.11, f32[16,16,128]{2,1,0:T(8,128)} %get-tuple-element.153.refs_4_, ...), custom_call_target="tpu_custom_call" | custom-call | tf_op jit(solution)/shard_map/weight_gradient/pallas_call | solution.py:306
  418.5 2.6 modes_to_cells.6
  421.1 3.7 all-to-all-start.7
  425.6 6.7 %weight_gradient.3 = (f32[2,32,32,8,128]{4,3,2,1,0:T(8,128)}, f32[8,128]{1,0:T(8,128)}) custom-call(f32[16,16,128]{2,1,0:T(8,128)} %get-tuple-element.143.refs_0_, f32[16,16,128]{2,1,0:T(8,128)} %copy-done.9, f32[16,16,128]{2,1,0:T(8,128)} %copy-done.10, f32[16,16,128]{2,1,0:T(8,128)} %copy-done.11, ...), custom_call_target="tpu_custom_call", output_to_operand_aliasing={{0}: (12, {})} | custom-call | tf_op jit(solution)/shard_map/weight_gradient/pallas_call | solution.py:306
  432.3 26.7 %collective-permute-done.27.refs_1_ = f32[4,16,16,128]{3,2,1,0:T(8,128)S(1)} collective-permute-done((f32[4,16,16,128]{3,2,1,0:T(8,128)S(1)}, f32[4,16,16,128]{3,2,1,0:T(8,128)S(1)}, u32[]{:S(2)}, u32[]{:S(2)}) %collective-permute-start.27) | collective-permute-done | bytes 524320 | tf_op jit(solution)/shard_map/ppermute | solution.py:712
  459.7 2.7 modes_to_cells.7
  463.7 5.2 %all-to-all-start.6 = ((f32[4,2,16,32,128]{4,3,2,1,0:T(8,128)}), f32[4,2,16,32,128]{4,3,2,1,0:T(8,128)}, u32[]{:S(2)}, u32[]{:S(2)}) async-start(f32[4,2,16,32,128]{4,3,2,1,0:T(8,128)} %get-tuple-element.172), calls=%async_computation.6 | async-start | bytes 4194304 | tf_op jit(solution)/shard_map/all_to_all | solution.py:680
  468.9 15.8 %modes_to_planes.2 = (f32[1,32,16,128,128]{4,3,2,1,0:T(8,128)}, f32[8,128]{1,0:T(8,128)}) custom-call(f32[8,16,32,128]{3,2,1,0:T(8,128)} %bitcast.33, f32[1,32,16,128,128]{4,3,2,1,0:T(8,128)} %get-tuple-element.174.refs_1_, bf16[768,1024]{1,0:T(8,128)(2,1)} %constant.68.clone.refs_2_, ...), custom_call_target="tpu_custom_call", output_to_operand_aliasing={{0}: (1, {})} | custom-call | tf_op jit(solution)/shard_map/modes_to_planes/pallas_call | solution.py:306
  484.8 9.2 %all-to-all-done.6 = f32[4,2,16,32,128]{4,3,2,1,0:T(8,128)} async-done(((f32[4,2,16,32,128]{4,3,2,1,0:T(8,128)}), f32[4,2,16,32,128]{4,3,2,1,0:T(8,128)}, u32[]{:S(2)}, u32[]{:S(2)}) %all-to-all-start.6) | async-done | bytes 2097184 | tf_op jit(solution)/shard_map/all_to_all | solution.py:680
  494.0 15.8 %modes_to_planes.3 = (f32[1,32,16,128,128]{4,3,2,1,0:T(8,128)}, f32[8,128]{1,0:T(8,128)}) custom-call(f32[8,16,32,128]{3,2,1,0:T(8,128)} %bitcast.27.refs_0_, f32[1,32,16,128,128]{4,3,2,1,0:T(8,128)} %get-tuple-element.176.refs_1_, bf16[768,1024]{1,0:T(8,128)(2,1)} %constant.68.clone.refs_2_, ...), custom_call_target="tpu_custom_call", output_to_operand_aliasing={{0}: (1, {})} | custom-call | tf_op jit(solution)/shard_map/modes_to_planes/pallas_call | solution.py:306
  (145 shorter events, 78.8 us)
Async XLA Ops:
  14.4 30.1 %all-to-all-start = ((f32[4,2,16,32,128]{4,3,2,1,0:T(8,128)}), f32[4,2,16,32,128]{4,3,2,1,0:T(8,128)S(1)}, u32[]{:S(2)}, u32[]{:S(2)}) async-start(f32[4,2,16,32,128]{4,3,2,1,0:T(8,128)} %bitcast.38), calls=%async_computation | async-start | bytes 4194304 | tf_op jit(solution)/shard_map/all_to_all | solution.py:680
  45.9 41.0 %all-to-all-start.1 = ((f32[4,2,16,32,128]{4,3,2,1,0:T(8,128)}), f32[4,2,16,32,128]{4,3,2,1,0:T(8,128)S(1)}, u32[]{:S(2)}, u32[]{:S(2)}) async-start(f32[4,2,16,32,128]{4,3,2,1,0:T(8,128)} %bitcast.35), calls=%async_computation.1 | async-start | bytes 4194304 | tf_op jit(solution)/shard_map/all_to_all | solution.py:680
  75.1 38.4 %collective-permute-start = (f32[16,64,128]{2,1,0:T(8,128)}, f32[16,64,128]{2,1,0:T(8,128)S(1)}, u32[]{:S(2)}, u32[]{:S(2)}) collective-permute-start(f32[16,64,128]{2,1,0:T(8,128)} %get-tuple-element.97), channel_id=1, source_target_pairs={{0,4},{1,5},{2,6},{3,7},{4,0},{5,1},{6,2},{7,3},{8,12},{9,13},{10,... | collective-permute-start | bytes 1572872 | tf_op jit(solution)/shard_map/ppermute | solution.py:704
  90.5 37.2 %collective-permute-start.4 = (f32[16,64,128]{2,1,0:T(8,128)}, f32[16,64,128]{2,1,0:T(8,128)S(1)}, u32[]{:S(2)}, u32[]{:S(2)}) collective-permute-start(f32[16,64,128]{2,1,0:T(8,128)} %get-tuple-element.107), channel_id=1, source_target_pairs={{0,4},{1,5},{2,6},{3,7},{4,0},{5,1},{6,2},{7,3},{8,12},{9,13},{10,... | collective-permute-start | bytes 1572872 | tf_op jit(solution)/shard_map/ppermute | solution.py:704
  116.7 16.2 %collective-permute-start.1 = (f32[16,16,128]{2,1,0:T(8,128)}, f32[16,16,128]{2,1,0:T(8,128)S(1)}, u32[]{:S(2)}, u32[]{:S(2)}) collective-permute-start(f32[16,16,128]{2,1,0:T(8,128)} %get-tuple-element.104), channel_id=1, source_target_pairs={{0,8},{8,0},{16,24},{24,16},{1,9},{9,1},{17,25},{25,17},{2,10},{10... | collective-permute-start | bytes 393224 | tf_op jit(solution)/shard_map/ppermute | solution.py:686
  116.7 16.2 %collective-permute-start.2 = (f32[16,16,128]{2,1,0:T(8,128)}, f32[16,16,128]{2,1,0:T(8,128)S(1)}, u32[]{:S(2)}, u32[]{:S(2)}) collective-permute-start(f32[16,16,128]{2,1,0:T(8,128)} %get-tuple-element.105), channel_id=1, source_target_pairs={{0,16},{8,24},{16,0},{24,8},{1,17},{9,25},{17,1},{25,9},{2,18},{10... | collective-permute-start | bytes 393224 | tf_op jit(solution)/shard_map/ppermute | solution.py:686
  118.3 14.6 %collective-permute-start.3 = (f32[16,16,128]{2,1,0:T(8,128)}, f32[16,16,128]{2,1,0:T(8,128)S(1)}, u32[]{:S(2)}, u32[]{:S(2)}) collective-permute-start(f32[16,16,128]{2,1,0:T(8,128)} %get-tuple-element.106), channel_id=1, source_target_pairs={{0,24},{8,16},{16,8},{24,0},{1,25},{9,17},{17,9},{25,1},{2,26},{10... | collective-permute-start | bytes 393224 | tf_op jit(solution)/shard_map/ppermute | solution.py:686
  130.9 2.0 collective-permute-start.5
  131.3 6.5 %collective-permute-start.6 = (f32[16,16,128]{2,1,0:T(8,128)}, f32[16,16,128]{2,1,0:T(8,128)S(1)}, u32[]{:S(2)}, u32[]{:S(2)}) collective-permute-start(f32[16,16,128]{2,1,0:T(8,128)} %get-tuple-element.113), channel_id=1, source_target_pairs={{0,16},{8,24},{16,0},{24,8},{1,17},{9,25},{17,1},{25,9},{2,18},{10... | collective-permute-start | bytes 393224 | tf_op jit(solution)/shard_map/ppermute | solution.py:686
  132.9 6.3 %copy-start.19 = (f32[16,16,128]{2,1,0:T(8,128)}, f32[16,16,128]{2,1,0:T(8,128)S(1)}, u32[]{:S(2)}) copy-start(f32[16,16,128]{2,1,0:T(8,128)S(1)} %collective-permute-done.1.refs_1_.refs_9_) | copy-start | bytes 393220
  132.9 6.3 %collective-permute-start.7 = (f32[16,16,128]{2,1,0:T(8,128)}, f32[16,16,128]{2,1,0:T(8,128)S(1)}, u32[]{:S(2)}, u32[]{:S(2)}) collective-permute-start(f32[16,16,128]{2,1,0:T(8,128)} %get-tuple-element.114), channel_id=1, source_target_pairs={{0,24},{8,16},{16,8},{24,0},{1,25},{9,17},{17,9},{25,1},{2,26},{10... | collective-permute-start | bytes 393224 | tf_op jit(solution)/shard_map/ppermute | solution.py:686
  132.9 6.2 %copy-start.20 = (f32[16,16,128]{2,1,0:T(8,128)}, f32[16,16,128]{2,1,0:T(8,128)S(1)}, u32[]{:S(2)}) copy-start(f32[16,16,128]{2,1,0:T(8,128)S(1)} %collective-permute-done.2.refs_2_.refs_10_) | copy-start | bytes 393220
  132.9 6.2 %copy-start.21 = (f32[16,16,128]{2,1,0:T(8,128)}, f32[16,16,128]{2,1,0:T(8,128)S(1)}, u32[]{:S(2)}) copy-start(f32[16,16,128]{2,1,0:T(8,128)S(1)} %collective-permute-done.3.refs_3_.refs_11_) | copy-start | bytes 393220
  145.7 2.2 collective-permute-start.8
  146.3 6.6 %collective-permute-start.9 = (f32[16,16,128]{2,1,0:T(8,128)}, f32[16,16,128]{2,1,0:T(8,128)S(1)}, u32[]{:S(2)}, u32[]{:S(2)}) collective-permute-start(f32[16,16,128]{2,1,0:T(8,128)} %get-tuple-element.118), channel_id=1, source_target_pairs={{0,16},{8,24},{16,0},{24,8},{1,17},{9,25},{17,1},{25,9},{2,18},{10... | collective-permute-start | bytes 393224 | tf_op jit(solution)/shard_map/ppermute | solution.py:686
  147.8 6.1 %collective-permute-start.10 = (f32[16,16,128]{2,1,0:T(8,128)}, f32[16,16,128]{2,1,0:T(8,128)S(1)}, u32[]{:S(2)}, u32[]{:S(2)}) collective-permute-start(f32[16,16,128]{2,1,0:T(8,128)} %get-tuple-element.119), channel_id=1, source_target_pairs={{0,24},{8,16},{16,8},{24,0},{1,25},{9,17},{17,9},{25,1},{2,26},{10... | collective-permute-start | bytes 393224 | tf_op jit(solution)/shard_map/ppermute | solution.py:686
  154.9 25.7 %collective-permute-start.11 = (f32[4,16,16,128]{3,2,1,0:T(8,128)S(1)}, f32[4,16,16,128]{3,2,1,0:T(8,128)S(1)}, u32[]{:S(2)}, u32[]{:S(2)}) collective-permute-start(f32[4,16,16,128]{3,2,1,0:T(8,128)S(1)} %pad_maximum_fusion.refs_0_), channel_id=1, source_target_pairs={{0,4},{1,5},{2,6},{3,7},{4,0},{5,1},{6,2},{7,3},{8,12},{9,13},{10,... | collective-permute-start | bytes 1572872 | tf_op jit(solution)/shard_map/ppermute | solution.py:712
  161.0 3.8 collective-permute-start.12
  161.8 6.6 %collective-permute-start.13 = (f32[16,16,128]{2,1,0:T(8,128)}, f32[16,16,128]{2,1,0:T(8,128)S(1)}, u32[]{:S(2)}, u32[]{:S(2)}) collective-permute-start(f32[16,16,128]{2,1,0:T(8,128)} %get-tuple-element.124), channel_id=1, source_target_pairs={{0,16},{8,24},{16,0},{24,8},{1,17},{9,25},{17,1},{25,9},{2,18},{10... | collective-permute-start | bytes 393224 | tf_op jit(solution)/shard_map/ppermute | solution.py:686
  163.3 6.1 %collective-permute-start.14 = (f32[16,16,128]{2,1,0:T(8,128)}, f32[16,16,128]{2,1,0:T(8,128)S(1)}, u32[]{:S(2)}, u32[]{:S(2)}) collective-permute-start(f32[16,16,128]{2,1,0:T(8,128)} %get-tuple-element.125), channel_id=1, source_target_pairs={{0,24},{8,16},{16,8},{24,0},{1,25},{9,17},{17,9},{25,1},{2,26},{10... | collective-permute-start | bytes 393224 | tf_op jit(solution)/shard_map/ppermute | solution.py:686
  184.0 41.6 %all-to-all-start.2 = ((f32[4,2,16,32,128]{4,3,2,1,0:T(8,128)}), f32[4,2,16,32,128]{4,3,2,1,0:T(8,128)S(1)}, u32[]{:S(2)}, u32[]{:S(2)}) async-start(f32[4,2,16,32,128]{4,3,2,1,0:T(8,128)} %get-tuple-element.126), calls=%async_computation.2 | async-start | bytes 4194304 | tf_op jit(solution)/shard_map/all_to_all | solution.py:680
  187.8 34.4 %collective-permute-start.15 = (f32[4,16,16,128]{3,2,1,0:T(8,128)S(1)}, f32[4,16,16,128]{3,2,1,0:T(8,128)S(1)}, u32[]{:S(2)}, u32[]{:S(2)}) collective-permute-start(f32[4,16,16,128]{3,2,1,0:T(8,128)S(1)} %copy-done.8), channel_id=1, source_target_pairs={{0,4},{1,5},{2,6},{3,7},{4,0},{5,1},{6,2},{7,3},{8,12},{9,13},{10,... | collective-permute-start | bytes 1572872 | tf_op jit(solution)/shard_map/ppermute | solution.py:712
  227.0 34.4 %all-to-all-start.4 = ((f32[4,2,16,32,128]{4,3,2,1,0:T(8,128)}), f32[4,2,16,32,128]{4,3,2,1,0:T(8,128)}, u32[]{:S(2)}, u32[]{:S(2)}) async-start(f32[4,2,16,32,128]{4,3,2,1,0:T(8,128)} %get-tuple-element.131), calls=%async_computation.4 | async-start | bytes 4194304 | tf_op jit(solution)/shard_map/all_to_all | solution.py:680
  261.4 33.8 %all-to-all-start.3 = ((f32[4,2,16,32,128]{4,3,2,1,0:T(8,128)}), f32[4,2,16,32,128]{4,3,2,1,0:T(8,128)S(1)}, u32[]{:S(2)}, u32[]{:S(2)}) async-start(f32[4,2,16,32,128]{4,3,2,1,0:T(8,128)} %bitcast.37), calls=%async_computation.3 | async-start | bytes 4194304 | tf_op jit(solution)/shard_map/all_to_all | solution.py:680
  296.5 40.1 %all-to-all-start.5 = ((f32[4,2,16,32,128]{4,3,2,1,0:T(8,128)}), f32[4,2,16,32,128]{4,3,2,1,0:T(8,128)S(1)}, u32[]{:S(2)}, u32[]{:S(2)}) async-start(f32[4,2,16,32,128]{4,3,2,1,0:T(8,128)} %bitcast.36), calls=%async_computation.5 | async-start | bytes 4194304 | tf_op jit(solution)/shard_map/all_to_all | solution.py:680
  303.0 37.3 %collective-permute-start.16 = (f32[16,64,128]{2,1,0:T(8,128)}, f32[16,64,128]{2,1,0:T(8,128)S(1)}, u32[]{:S(2)}, u32[]{:S(2)}) collective-permute-start(f32[16,64,128]{2,1,0:T(8,128)} %get-tuple-element.135), channel_id=1, source_target_pairs={{0,4},{1,5},{2,6},{3,7},{4,0},{5,1},{6,2},{7,3},{8,12},{9,13},{10,... | collective-permute-start | bytes 1572872 | tf_op jit(solution)/shard_map/ppermute | solution.py:704
  340.3 23.8 %collective-permute-start.20 = (f32[16,64,128]{2,1,0:T(8,128)}, f32[16,64,128]{2,1,0:T(8,128)S(1)}, u32[]{:S(2)}, u32[]{:S(2)}) collective-permute-start(f32[16,64,128]{2,1,0:T(8,128)} %get-tuple-element.147), channel_id=1, source_target_pairs={{0,4},{1,5},{2,6},{3,7},{4,0},{5,1},{6,2},{7,3},{8,12},{9,13},{10,... | collective-permute-start | bytes 1572872 | tf_op jit(solution)/shard_map/ppermute | solution.py:704
  343.4 25.4 %collective-permute-start.17 = (f32[16,16,128]{2,1,0:T(8,128)}, f32[16,16,128]{2,1,0:T(8,128)S(1)}, u32[]{:S(2)}, u32[]{:S(2)}) collective-permute-start(f32[16,16,128]{2,1,0:T(8,128)} %get-tuple-element.144), channel_id=1, source_target_pairs={{0,8},{8,0},{16,24},{24,16},{1,9},{9,1},{17,25},{25,17},{2,10},{10... | collective-permute-start | bytes 393224 | tf_op jit(solution)/shard_map/ppermute | solution.py:686
  343.4 25.6 %collective-permute-start.18 = (f32[16,16,128]{2,1,0:T(8,128)}, f32[16,16,128]{2,1,0:T(8,128)S(1)}, u32[]{:S(2)}, u32[]{:S(2)}) collective-permute-start(f32[16,16,128]{2,1,0:T(8,128)} %get-tuple-element.145), channel_id=1, source_target_pairs={{0,16},{8,24},{16,0},{24,8},{1,17},{9,25},{17,1},{25,9},{2,18},{10... | collective-permute-start | bytes 393224 | tf_op jit(solution)/shard_map/ppermute | solution.py:686
  345.1 24.0 %collective-permute-start.19 = (f32[16,16,128]{2,1,0:T(8,128)}, f32[16,16,128]{2,1,0:T(8,128)S(1)}, u32[]{:S(2)}, u32[]{:S(2)}) collective-permute-start(f32[16,16,128]{2,1,0:T(8,128)} %get-tuple-element.146), channel_id=1, source_target_pairs={{0,24},{8,16},{16,8},{24,0},{1,25},{9,17},{17,9},{25,1},{2,26},{10... | collective-permute-start | bytes 393224 | tf_op jit(solution)/shard_map/ppermute | solution.py:686
  367.2 1.9 collective-permute-start.21
  367.2 6.6 %collective-permute-start.22 = (f32[16,16,128]{2,1,0:T(8,128)}, f32[16,16,128]{2,1,0:T(8,128)S(1)}, u32[]{:S(2)}, u32[]{:S(2)}) collective-permute-start(f32[16,16,128]{2,1,0:T(8,128)} %get-tuple-element.155), channel_id=1, source_target_pairs={{0,16},{8,24},{16,0},{24,8},{1,17},{9,25},{17,1},{25,9},{2,18},{10... | collective-permute-start | bytes 393224 | tf_op jit(solution)/shard_map/ppermute | solution.py:686
  368.9 6.8 %copy-start.9 = (f32[16,16,128]{2,1,0:T(8,128)}, f32[16,16,128]{2,1,0:T(8,128)S(1)}, u32[]{:S(2)}) copy-start(f32[16,16,128]{2,1,0:T(8,128)S(1)} %collective-permute-done.17.refs_1_) | copy-start | bytes 393220
  368.9 6.8 %collective-permute-start.23 = (f32[16,16,128]{2,1,0:T(8,128)}, f32[16,16,128]{2,1,0:T(8,128)S(1)}, u32[]{:S(2)}, u32[]{:S(2)}) collective-permute-start(f32[16,16,128]{2,1,0:T(8,128)} %get-tuple-element.156), channel_id=1, source_target_pairs={{0,24},{8,16},{16,8},{24,0},{1,25},{9,17},{17,9},{25,1},{2,26},{10... | collective-permute-start | bytes 393224 | tf_op jit(solution)/shard_map/ppermute | solution.py:686
  369.1 6.6 %copy-start.10 = (f32[16,16,128]{2,1,0:T(8,128)}, f32[16,16,128]{2,1,0:T(8,128)S(1)}, u32[]{:S(2)}) copy-start(f32[16,16,128]{2,1,0:T(8,128)S(1)} %collective-permute-done.18.refs_2_) | copy-start | bytes 393220
  369.1 6.6 %copy-start.11 = (f32[16,16,128]{2,1,0:T(8,128)}, f32[16,16,128]{2,1,0:T(8,128)S(1)}, u32[]{:S(2)}) copy-start(f32[16,16,128]{2,1,0:T(8,128)S(1)} %collective-permute-done.19.refs_3_) | copy-start | bytes 393220
  369.1 6.6 %copy-start.12 = (f32[16,16,128]{2,1,0:T(8,128)}, f32[16,16,128]{2,1,0:T(8,128)S(1)}, u32[]{:S(2)}) copy-start(f32[16,16,128]{2,1,0:T(8,128)S(1)} %collective-permute-done.21.refs_5_) | copy-start | bytes 393220
  381.9 1.9 collective-permute-start.28
  382.2 6.5 %collective-permute-start.29 = (f32[16,16,128]{2,1,0:T(8,128)}, f32[16,16,128]{2,1,0:T(8,128)S(1)}, u32[]{:S(2)}, u32[]{:S(2)}) collective-permute-start(f32[16,16,128]{2,1,0:T(8,128)} %get-tuple-element.166), channel_id=1, source_target_pairs={{0,16},{8,24},{16,0},{24,8},{1,17},{9,25},{17,1},{25,9},{2,18},{10... | collective-permute-start | bytes 393224 | tf_op jit(solution)/shard_map/ppermute | solution.py:686
  383.8 6.4 %collective-permute-start.30 = (f32[16,16,128]{2,1,0:T(8,128)}, f32[16,16,128]{2,1,0:T(8,128)S(1)}, u32[]{:S(2)}, u32[]{:S(2)}) collective-permute-start(f32[16,16,128]{2,1,0:T(8,128)} %get-tuple-element.167), channel_id=1, source_target_pairs={{0,24},{8,16},{16,8},{24,0},{1,25},{9,17},{17,9},{25,1},{2,26},{10... | collective-permute-start | bytes 393224 | tf_op jit(solution)/shard_map/ppermute | solution.py:686
  391.1 7.9 %copy-start.6 = (f32[4,16,16,128]{3,2,1,0:T(8,128)}, f32[4,16,16,128]{3,2,1,0:T(8,128)S(1)}, u32[]{:S(2)}) copy-start(f32[4,16,16,128]{3,2,1,0:T(8,128)S(1)} %pad_maximum_fusion.3.refs_13_.refs_0_) | copy-start | bytes 1572868
  391.1 26.6 %collective-permute-start.31 = (f32[4,16,16,128]{3,2,1,0:T(8,128)S(1)}, f32[4,16,16,128]{3,2,1,0:T(8,128)S(1)}, u32[]{:S(2)}, u32[]{:S(2)}) collective-permute-start(f32[4,16,16,128]{3,2,1,0:T(8,128)S(1)} %pad_maximum_fusion.3.refs_13_.refs_0_), channel_id=1, source_target_pairs={{0,4},{1,5},{2,6},{3,7},{4,0},{5,1},{6,2},{7,3},{8,12},{9,13},{10,... | collective-permute-start | bytes 1572872 | tf_op jit(solution)/shard_map/ppermute | solution.py:712
  399.0 2.0 collective-permute-start.24
  399.4 6.6 %collective-permute-start.25 = (f32[16,16,128]{2,1,0:T(8,128)}, f32[16,16,128]{2,1,0:T(8,128)S(1)}, u32[]{:S(2)}, u32[]{:S(2)}) collective-permute-start(f32[16,16,128]{2,1,0:T(8,128)} %get-tuple-element.161), channel_id=1, source_target_pairs={{0,16},{8,24},{16,0},{24,8},{1,17},{9,25},{17,1},{25,9},{2,18},{10... | collective-permute-start | bytes 393224 | tf_op jit(solution)/shard_map/ppermute | solution.py:686
  400.9 6.2 %collective-permute-start.26 = (f32[16,16,128]{2,1,0:T(8,128)}, f32[16,16,128]{2,1,0:T(8,128)S(1)}, u32[]{:S(2)}, u32[]{:S(2)}) collective-permute-start(f32[16,16,128]{2,1,0:T(8,128)} %get-tuple-element.162), channel_id=1, source_target_pairs={{0,24},{8,16},{16,8},{24,0},{1,25},{9,17},{17,9},{25,1},{2,26},{10... | collective-permute-start | bytes 393224 | tf_op jit(solution)/shard_map/ppermute | solution.py:686
  421.1 41.3 %all-to-all-start.7 = ((f32[4,2,16,32,128]{4,3,2,1,0:T(8,128)}), f32[4,2,16,32,128]{4,3,2,1,0:T(8,128)S(1)}, u32[]{:S(2)}, u32[]{:S(2)}) async-start(f32[4,2,16,32,128]{4,3,2,1,0:T(8,128)} %get-tuple-element.173), calls=%async_computation.7 | async-start | bytes 4194304 | tf_op jit(solution)/shard_map/all_to_all | solution.py:680
  424.8 34.1 %collective-permute-start.27 = (f32[4,16,16,128]{3,2,1,0:T(8,128)S(1)}, f32[4,16,16,128]{3,2,1,0:T(8,128)S(1)}, u32[]{:S(2)}, u32[]{:S(2)}) collective-permute-start(f32[4,16,16,128]{3,2,1,0:T(8,128)S(1)} %copy-done.7), channel_id=1, source_target_pairs={{0,4},{1,5},{2,6},{3,7},{4,0},{5,1},{6,2},{7,3},{8,12},{9,13},{10,... | collective-permute-start | bytes 1572872 | tf_op jit(solution)/shard_map/ppermute | solution.py:712
  463.7 30.3 %all-to-all-start.6 = ((f32[4,2,16,32,128]{4,3,2,1,0:T(8,128)}), f32[4,2,16,32,128]{4,3,2,1,0:T(8,128)}, u32[]{:S(2)}, u32[]{:S(2)}) async-start(f32[4,2,16,32,128]{4,3,2,1,0:T(8,128)} %get-tuple-element.172), calls=%async_computation.6 | async-start | bytes 4194304 | tf_op jit(solution)/shard_map/all_to_all | solution.py:680
  (25 other events, 54.9 us)

commit v2 on v1

--- a/solution.py
+++ b/solution.py
@@ -734,10 +734,10 @@
 
     map_fields = partial(channels, fields, point, "point")
     forward(0)
+    map_fields(0)
     forward(1)
-    map_fields(0)
+    send(0)
     map_fields(1)
-    send(0)
     map_fields(2)
     send(1)
     keep(0)
@@ -764,9 +764,9 @@
     mixed(1, gradients, True)
     weights(0, state["own", 0][0], state["own", 1][0])
     back(0)
-    weights(1)
     back(1)
     final(0)
+    weights(1)
     final(1)
     return state["result"], state["weights"]
 

time: 513 us -> 499 us (0.973)
  waiting for transfers between devices: 163 us -> 145 us
    ppermute x4, waiting for transfers between devices: 23.1 us -> 9.56 us  [send(): lax.ppermute(line_send(order, state['near', q], tx), 'mp', across)]
    all_to_all x8, waiting for transfers between devices: 31.9 us -> 21.8 us  [swap_near(): lax.all_to_all(data, 'mp', split_axis=0, concat_axis=0, axis_index_groups...]
    ppermute x4, waiting for transfers between devices: 72 us -> 77.4 us  [mixed(): state['own', q] = (own, lax.ppermute(own, 'mp', across))]
    unnamed x67 -> x69, local copies, waits for them, and re-layouts: 16.3 us -> 17.6 us
  transfers between devices with their start and end apart: 40 -> 40, of which waited for: 21 -> 20; matrix products, arithmetic and copies ran while one was open for 2% -> 2% of each run, Pallas kernels for 42% -> 43%
where the time goes in v2:
time: 499 us; the launch traced here: 496 us
  Pallas kernels  257 us (52%)
  waiting for transfers between devices  145 us (29%)
  starting transfers between devices  63.7 us (13%)
  local copies, waits for them, and re-layouts  24.2 us (5%)
  other arithmetic  5.35 us (1%)
    pallas_call x32, Pallas kernels, call(): pl.pallas_call(body, grid=grid, in_specs=list(in_specs) + [anywhere] * le...  253 us
    ppermute x4, waiting for transfers between devices, mixed(): state['own', q] = (own, lax.ppermute(own, 'mp', across))  77.4 us
    all_to_all x8, starting transfers between devices, swap_near(): lax.all_to_all(data, 'mp', split_axis=0, concat_axis=0, axis_index_groups...  37 us
    ppermute x24, waiting for transfers between devices, swap_groups(): lax.ppermute(pieces[k], 'dp', [(j, j ^ k) for j in range(groups)])  36.1 us
    all_to_all x8, waiting for transfers between devices, swap_near(): lax.all_to_all(data, 'mp', split_axis=0, concat_axis=0, axis_index_groups...  21.8 us
    unnamed x69, local copies, waits for them, and re-layouts  17.6 us
    ppermute x24, starting transfers between devices, swap_groups(): lax.ppermute(pieces[k], 'dp', [(j, j ^ k) for j in range(groups)])  15.7 us
  transfers between devices with their start and end apart: 40, of which 20 were waited for; matrix products, arithmetic and copies ran while one was open for 2% of the time, Pallas kernels for 43%

profile of v2, /device:TPU:0, one launch (start us, length us, event | category | flops | bytes accessed | tf_op | source)
XLA Modules:
  0.0 496.2 jit_solution(5947056715967312548)
XLA Ops:
  2.1 12.3 %planes_to_modes.2 = (f32[8,16,32,128]{3,2,1,0:T(8,128)}, f32[8,128]{1,0:T(8,128)}) custom-call(f32[1,32,16,128,128]{4,3,2,1,0:T(8,128)} %refs_0_.11, bf16[128,256]{1,0:T(8,128)(2,1)} %dynamic-slice_bitcast_fusion.2.refs_1_.refs_5_, bf16[3072,256]{1,0:T(8,128)(2,1)} %constant.66.clone.refs_2_), custom_call_target="tpu_custom_call" | custom-call | tf_op jit(solution)/shard_map/planes_to_modes/pallas_call | solution.py:306
  14.4 5.4 %all-to-all-start = ((f32[4,2,16,32,128]{4,3,2,1,0:T(8,128)}), f32[4,2,16,32,128]{4,3,2,1,0:T(8,128)S(1)}, u32[]{:S(2)}, u32[]{:S(2)}) async-start(f32[4,2,16,32,128]{4,3,2,1,0:T(8,128)} %bitcast.39), calls=%async_computation | async-start | bytes 4194304 | tf_op jit(solution)/shard_map/all_to_all | solution.py:680
  23.3 9.2 %channel_map.8 = (f32[1,32,16,128,128]{4,3,2,1,0:T(8,128)}, f32[8,128]{1,0:T(8,128)}) custom-call(f32[1,32,16,128,128]{4,3,2,1,0:T(8,128)} %refs_0_.11, bf16[256,768]{1,0:T(8,128)(2,1)} %channel_table.2.refs_1_, f32[256,128]{1,0:T(8,128)} %broadcast_in_dim.15.refs_2_, f32[8,128]{1,0:T(8,128)} %get-tuple-element.92.refs_3_), custom_call_target="tpu_custom_call" | custom-call | tf_op jit(solution)/shard_map/channel_map/pallas_call | solution.py:306
  32.5 12.3 %planes_to_modes.3 = (f32[8,16,32,128]{3,2,1,0:T(8,128)}, f32[8,128]{1,0:T(8,128)}) custom-call(f32[1,32,16,128,128]{4,3,2,1,0:T(8,128)} %refs_0_.11, bf16[128,256]{1,0:T(8,128)(2,1)} %dynamic-slice_bitcast_fusion.2.refs_1_.refs_5_, bf16[3072,256]{1,0:T(8,128)(2,1)} %constant.66.clone.refs_2_, f32[8,128]{1,0:T(8,128)} %get-tuple-element.93.refs_3_), custom_call_target="tpu_custom_call" | custom-call | tf_op jit(solution)/shard_map/planes_to_modes/pallas_call | solution.py:306
  46.1 4.2 all-to-all-start.1
  54.0 2.6 collective-permute-start
  56.6 9.2 %channel_map.9 = (f32[1,32,16,128,128]{4,3,2,1,0:T(8,128)}, f32[8,128]{1,0:T(8,128)}) custom-call(f32[1,32,16,128,128]{4,3,2,1,0:T(8,128)} %refs_0_.11, bf16[256,768]{1,0:T(8,128)(2,1)} %channel_table.2.refs_1_, f32[256,128]{1,0:T(8,128)} %broadcast_in_dim.15.refs_2_, ...), custom_call_target="tpu_custom_call", output_to_operand_aliasing={{0}: (3, {})} | custom-call | tf_op jit(solution)/shard_map/channel_map/pallas_call | solution.py:306
  65.7 9.1 %channel_map.10 = (f32[1,32,16,128,128]{4,3,2,1,0:T(8,128)}, f32[8,128]{1,0:T(8,128)}) custom-call(f32[1,32,16,128,128]{4,3,2,1,0:T(8,128)} %refs_0_.11, bf16[256,768]{1,0:T(8,128)(2,1)} %channel_table.2.refs_1_, f32[256,128]{1,0:T(8,128)} %broadcast_in_dim.15.refs_2_, ...), custom_call_target="tpu_custom_call", output_to_operand_aliasing={{0}: (3, {})} | custom-call | tf_op jit(solution)/shard_map/channel_map/pallas_call | solution.py:306
  74.9 11.0 %all-to-all-done.1.refs_0_ = f32[4,2,16,32,128]{4,3,2,1,0:T(8,128)S(1)} async-done(((f32[4,2,16,32,128]{4,3,2,1,0:T(8,128)}), f32[4,2,16,32,128]{4,3,2,1,0:T(8,128)S(1)}, u32[]{:S(2)}, u32[]{:S(2)}) %all-to-all-start.1) | async-done | bytes 2097184 | tf_op jit(solution)/shard_map/all_to_all | solution.py:680
  90.8 2.4 own_modes.4
  95.1 9.1 %channel_map.11 = (f32[1,32,16,128,128]{4,3,2,1,0:T(8,128)}, f32[8,128]{1,0:T(8,128)}) custom-call(f32[1,32,16,128,128]{4,3,2,1,0:T(8,128)} %refs_0_.11, bf16[256,768]{1,0:T(8,128)(2,1)} %channel_table.2.refs_1_, f32[256,128]{1,0:T(8,128)} %broadcast_in_dim.15.refs_2_, ...), custom_call_target="tpu_custom_call", output_to_operand_aliasing={{0}: (3, {})} | custom-call | tf_op jit(solution)/shard_map/channel_map/pallas_call | solution.py:306
  104.2 9.6 %collective-permute-done.4.refs_1_ = f32[16,64,128]{2,1,0:T(8,128)S(1)} collective-permute-done((f32[16,64,128]{2,1,0:T(8,128)}, f32[16,64,128]{2,1,0:T(8,128)S(1)}, u32[]{:S(2)}, u32[]{:S(2)}) %collective-permute-start.4) | collective-permute-done | bytes 524320 | tf_op jit(solution)/shard_map/ppermute | solution.py:704
  114.5 2.4 own_modes.5
  118.8 4.7 collective-permute-done.6.refs_6_.refs_10_
  126.1 5.9 %mix.2 = (f32[16,16,128]{2,1,0:T(8,128)}, f32[16,16,128]{2,1,0:T(8,128)}, f32[16,16,128]{2,1,0:T(8,128)}, f32[16,16,128]{2,1,0:T(8,128)}, f32[8,128]{1,0:T(8,128)}) custom-call(f32[16,16,128]{2,1,0:T(8,128)} %get-tuple-element.103.refs_0_.refs_8_, f32[16,16,128]{2,1,0:T(8,128)} %copy-done.20, f32[16,16,128]{2,1,0:T(8,128)} %copy-done.21, ...), custom_call_target="tpu_custom_call" | custom-call | tf_op jit(solution)/shard_map/mix/pallas_call | solution.py:306
  133.8 5.0 collective-permute-done.9
  141.2 6.0 %mix.3 = (f32[16,16,128]{2,1,0:T(8,128)}, f32[16,16,128]{2,1,0:T(8,128)}, f32[16,16,128]{2,1,0:T(8,128)}, f32[16,16,128]{2,1,0:T(8,128)}, f32[8,128]{1,0:T(8,128)}) custom-call(f32[16,16,128]{2,1,0:T(8,128)} %get-tuple-element.103.refs_0_.refs_8_, f32[16,16,128]{2,1,0:T(8,128)} %copy-done.20, f32[16,16,128]{2,1,0:T(8,128)} %copy-done.21, ...), custom_call_target="tpu_custom_call" | custom-call | tf_op jit(solution)/shard_map/mix/pallas_call | solution.py:306
  150.8 3.6 collective-permute-done.13
  157.2 9.6 %collective-permute-done.11.refs_1_ = f32[4,16,16,128]{3,2,1,0:T(8,128)S(1)} collective-permute-done((f32[4,16,16,128]{3,2,1,0:T(8,128)S(1)}, f32[4,16,16,128]{3,2,1,0:T(8,128)S(1)}, u32[]{:S(2)}, u32[]{:S(2)}) %collective-permute-start.11) | collective-permute-done | bytes 524320 | tf_op jit(solution)/shard_map/ppermute | solution.py:712
  167.6 2.6 modes_to_cells.4
  170.3 3.7 all-to-all-start.2
  175.2 33.2 %collective-permute-done.15.refs_1_ = f32[4,16,16,128]{3,2,1,0:T(8,128)S(1)} collective-permute-done((f32[4,16,16,128]{3,2,1,0:T(8,128)S(1)}, f32[4,16,16,128]{3,2,1,0:T(8,128)S(1)}, u32[]{:S(2)}, u32[]{:S(2)}) %collective-permute-start.15) | collective-permute-done | bytes 524320 | tf_op jit(solution)/shard_map/ppermute | solution.py:712
  209.2 2.6 modes_to_cells.5
  213.2 5.3 %all-to-all-start.4 = ((f32[4,2,16,32,128]{4,3,2,1,0:T(8,128)}), f32[4,2,16,32,128]{4,3,2,1,0:T(8,128)}, u32[]{:S(2)}, u32[]{:S(2)}) async-start(f32[4,2,16,32,128]{4,3,2,1,0:T(8,128)} %get-tuple-element.131), calls=%async_computation.4 | async-start | bytes 4194304 | tf_op jit(solution)/shard_map/all_to_all | solution.py:680
  219.1 29.0 %modes_to_gradient_to_modes.2 = (f32[1,32,16,128,128]{4,3,2,1,0:T(8,128)}, f32[8,16,32,128]{3,2,1,0:T(8,128)}, f32[8,128]{1,0:T(8,128)}) custom-call(f32[8,16,32,128]{3,2,1,0:T(8,128)} %bitcast.34, f32[1,32,16,128,128]{4,3,2,1,0:T(8,128)} %get-tuple-element.127.refs_1_, bf16[1,32,16,128,128]{4,3,2,1,0:T(8,128)(2,1)} %refs_2_.7, ...), custom_call_target="tpu_custom_call", output_to_operand_aliasing={{0}: (1, {})} | custom-call | tf_op jit(solution)/shard_map/modes_to_gradient_to_modes/pallas_call | solution.py:306
  248.1 4.6 all-to-all-start.3
  252.8 29.1 %modes_to_gradient_to_modes.3 = (f32[1,32,16,128,128]{4,3,2,1,0:T(8,128)}, f32[8,16,32,128]{3,2,1,0:T(8,128)}, f32[8,128]{1,0:T(8,128)}) custom-call(f32[8,16,32,128]{3,2,1,0:T(8,128)} %bitcast.17.refs_0_, f32[1,32,16,128,128]{4,3,2,1,0:T(8,128)} %get-tuple-element.132.refs_1_, ...), custom_call_target="tpu_custom_call", output_to_operand_aliasing={{0}: (1, {})} | custom-call | tf_op jit(solution)/shard_map/modes_to_gradient_to_modes/pallas_call | solution.py:306
  283.2 4.2 all-to-all-start.5
  294.3 9.2 %channel_map.12 = (f32[1,32,16,128,128]{4,3,2,1,0:T(8,128)}, f32[8,128]{1,0:T(8,128)}) custom-call(f32[1,32,16,128,128]{4,3,2,1,0:T(8,128)} %get-tuple-element.137.refs_0_, bf16[256,768]{1,0:T(8,128)(2,1)} %channel_table.3.refs_1_, f32[256,128]{1,0:T(8,128)} %broadcast_in_dim.16.refs_2_, f32[8,128]{1,0:T(8,128)} %get-tuple-element.138.refs_3_), custom_call_target="tpu_custom_call" | custom-call | tf_op jit(solution)/shard_map/channel_map/pallas_call | solution.py:306
  303.5 9.2 %channel_map.13 = (f32[1,32,16,128,128]{4,3,2,1,0:T(8,128)}, f32[8,128]{1,0:T(8,128)}) custom-call(f32[1,32,16,128,128]{4,3,2,1,0:T(8,128)} %get-tuple-element.137.refs_0_, bf16[256,768]{1,0:T(8,128)(2,1)} %channel_table.3.refs_1_, f32[256,128]{1,0:T(8,128)} %broadcast_in_dim.16.refs_2_, ...), custom_call_target="tpu_custom_call", output_to_operand_aliasing={{0}: (3, {})} | custom-call | tf_op jit(solution)/shard_map/channel_map/pallas_call | solution.py:306
  312.7 9.3 %all-to-all-done.5.refs_0_ = f32[4,2,16,32,128]{4,3,2,1,0:T(8,128)S(1)} async-done(((f32[4,2,16,32,128]{4,3,2,1,0:T(8,128)}), f32[4,2,16,32,128]{4,3,2,1,0:T(8,128)S(1)}, u32[]{:S(2)}, u32[]{:S(2)}) %all-to-all-start.5) | async-done | bytes 2097184 | tf_op jit(solution)/shard_map/all_to_all | solution.py:680
  331.2 9.2 %channel_map.14 = (f32[1,32,16,128,128]{4,3,2,1,0:T(8,128)}, f32[8,128]{1,0:T(8,128)}) custom-call(f32[1,32,16,128,128]{4,3,2,1,0:T(8,128)} %get-tuple-element.137.refs_0_, bf16[256,768]{1,0:T(8,128)(2,1)} %channel_table.3.refs_1_, f32[256,128]{1,0:T(8,128)} %broadcast_in_dim.16.refs_2_, ...), custom_call_target="tpu_custom_call", output_to_operand_aliasing={{0}: (3, {})} | custom-call | tf_op jit(solution)/shard_map/channel_map/pallas_call | solution.py:306
  340.4 9.2 %channel_map.15 = (f32[1,32,16,128,128]{4,3,2,1,0:T(8,128)}, f32[8,128]{1,0:T(8,128)}) custom-call(f32[1,32,16,128,128]{4,3,2,1,0:T(8,128)} %get-tuple-element.137.refs_0_, bf16[256,768]{1,0:T(8,128)(2,1)} %channel_table.3.refs_1_, f32[256,128]{1,0:T(8,128)} %broadcast_in_dim.16.refs_2_, ...), custom_call_target="tpu_custom_call", output_to_operand_aliasing={{0}: (3, {})} | custom-call | tf_op jit(solution)/shard_map/channel_map/pallas_call | solution.py:306
  354.7 5.0 collective-permute-done.22.refs_6_
  361.5 5.5 %mix_back.2 = (f32[16,16,128]{2,1,0:T(8,128)}, f32[16,16,128]{2,1,0:T(8,128)}, f32[16,16,128]{2,1,0:T(8,128)}, f32[16,16,128]{2,1,0:T(8,128)}, f32[8,128]{1,0:T(8,128)}) custom-call(f32[16,16,128]{2,1,0:T(8,128)} %get-tuple-element.143.refs_0_, f32[16,16,128]{2,1,0:T(8,128)} %copy-done.10, f32[16,16,128]{2,1,0:T(8,128)} %copy-done.11, ...), custom_call_target="tpu_custom_call" | custom-call | tf_op jit(solution)/shard_map/mix_back/pallas_call | solution.py:306
  369.2 5.1 %collective-permute-done.29 = f32[16,16,128]{2,1,0:T(8,128)S(1)} collective-permute-done((f32[16,16,128]{2,1,0:T(8,128)}, f32[16,16,128]{2,1,0:T(8,128)S(1)}, u32[]{:S(2)}, u32[]{:S(2)}) %collective-permute-start.29) | collective-permute-done | bytes 131104 | tf_op jit(solution)/shard_map/ppermute | solution.py:686
  376.3 2.6 collective-permute-start.31
  378.9 5.5 %mix_back.3 = (f32[16,16,128]{2,1,0:T(8,128)}, f32[16,16,128]{2,1,0:T(8,128)}, f32[16,16,128]{2,1,0:T(8,128)}, f32[16,16,128]{2,1,0:T(8,128)}, f32[8,128]{1,0:T(8,128)}) custom-call(f32[16,16,128]{2,1,0:T(8,128)} %get-tuple-element.143.refs_0_, f32[16,16,128]{2,1,0:T(8,128)} %copy-done.10, f32[16,16,128]{2,1,0:T(8,128)} %copy-done.11, ...), custom_call_target="tpu_custom_call" | custom-call | tf_op jit(solution)/shard_map/mix_back/pallas_call | solution.py:306
  386.4 5.0 %collective-permute-done.25 = f32[16,16,128]{2,1,0:T(8,128)S(1)} collective-permute-done((f32[16,16,128]{2,1,0:T(8,128)}, f32[16,16,128]{2,1,0:T(8,128)S(1)}, u32[]{:S(2)}, u32[]{:S(2)}) %collective-permute-start.25) | collective-permute-done | bytes 131104 | tf_op jit(solution)/shard_map/ppermute | solution.py:686
  394.4 6.7 %weight_gradient.2 = (f32[2,32,32,8,128]{4,3,2,1,0:T(8,128)}, f32[8,128]{1,0:T(8,128)}) custom-call(f32[16,16,128]{2,1,0:T(8,128)} %get-tuple-element.143.refs_0_, f32[16,16,128]{2,1,0:T(8,128)} %copy-done.10, f32[16,16,128]{2,1,0:T(8,128)} %copy-done.11, f32[16,16,128]{2,1,0:T(8,128)} %copy-done.12, f32[16,16,128]{2,1,0:T(8,128)} %get-tuple-element.153.refs_4_, ...), custom_call_target="tpu_custom_call" | custom-call | tf_op jit(solution)/shard_map/weight_gradient/pallas_call | solution.py:306
  403.8 2.7 modes_to_cells.6
  406.5 3.7 all-to-all-start.7
  411.7 32.7 %collective-permute-done.27.refs_1_ = f32[4,16,16,128]{3,2,1,0:T(8,128)S(1)} collective-permute-done((f32[4,16,16,128]{3,2,1,0:T(8,128)S(1)}, f32[4,16,16,128]{3,2,1,0:T(8,128)S(1)}, u32[]{:S(2)}, u32[]{:S(2)}) %collective-permute-start.27) | collective-permute-done | bytes 524320 | tf_op jit(solution)/shard_map/ppermute | solution.py:712
  445.2 2.6 modes_to_cells.7
  449.2 5.9 %all-to-all-start.6 = ((f32[4,2,16,32,128]{4,3,2,1,0:T(8,128)}), f32[4,2,16,32,128]{4,3,2,1,0:T(8,128)S(1)}, u32[]{:S(2)}, u32[]{:S(2)}) async-start(f32[4,2,16,32,128]{4,3,2,1,0:T(8,128)} %get-tuple-element.170), calls=%async_computation.6 | async-start | bytes 4194304 | tf_op jit(solution)/shard_map/all_to_all | solution.py:680
  455.1 15.8 %modes_to_planes.2 = (f32[1,32,16,128,128]{4,3,2,1,0:T(8,128)}, f32[8,128]{1,0:T(8,128)}) custom-call(f32[8,16,32,128]{3,2,1,0:T(8,128)} %bitcast.35, f32[1,32,16,128,128]{4,3,2,1,0:T(8,128)} %get-tuple-element.172.refs_1_, bf16[768,1024]{1,0:T(8,128)(2,1)} %constant.68.clone.refs_2_, ...), custom_call_target="tpu_custom_call", output_to_operand_aliasing={{0}: (1, {})} | custom-call | tf_op jit(solution)/shard_map/modes_to_planes/pallas_call | solution.py:306
  470.9 6.7 %weight_gradient.3 = (f32[2,32,32,8,128]{4,3,2,1,0:T(8,128)}, f32[8,128]{1,0:T(8,128)}) custom-call(f32[16,16,128]{2,1,0:T(8,128)} %get-tuple-element.143.refs_0_, f32[16,16,128]{2,1,0:T(8,128)} %copy-done.10, f32[16,16,128]{2,1,0:T(8,128)} %copy-done.11, f32[16,16,128]{2,1,0:T(8,128)} %copy-done.12, ...), custom_call_target="tpu_custom_call", output_to_operand_aliasing={{0}: (12, {})} | custom-call | tf_op jit(solution)/shard_map/weight_gradient/pallas_call | solution.py:306
  480.4 15.8 %modes_to_planes.3 = (f32[1,32,16,128,128]{4,3,2,1,0:T(8,128)}, f32[8,128]{1,0:T(8,128)}) custom-call(f32[8,16,32,128]{3,2,1,0:T(8,128)} %bitcast.33, f32[1,32,16,128,128]{4,3,2,1,0:T(8,128)} %get-tuple-element.174.refs_1_, bf16[768,1024]{1,0:T(8,128)(2,1)} %constant.68.clone.refs_2_, ...), custom_call_target="tpu_custom_call", output_to_operand_aliasing={{0}: (1, {})} | custom-call | tf_op jit(solution)/shard_map/modes_to_planes/pallas_call | solution.py:306
  (147 shorter events, 80.2 us)
Async XLA Ops:
  14.4 30.4 %all-to-all-start = ((f32[4,2,16,32,128]{4,3,2,1,0:T(8,128)}), f32[4,2,16,32,128]{4,3,2,1,0:T(8,128)S(1)}, u32[]{:S(2)}, u32[]{:S(2)}) async-start(f32[4,2,16,32,128]{4,3,2,1,0:T(8,128)} %bitcast.39), calls=%async_computation | async-start | bytes 4194304 | tf_op jit(solution)/shard_map/all_to_all | solution.py:680
  46.1 39.7 %all-to-all-start.1 = ((f32[4,2,16,32,128]{4,3,2,1,0:T(8,128)}), f32[4,2,16,32,128]{4,3,2,1,0:T(8,128)S(1)}, u32[]{:S(2)}, u32[]{:S(2)}) async-start(f32[4,2,16,32,128]{4,3,2,1,0:T(8,128)} %bitcast.36), calls=%async_computation.1 | async-start | bytes 4194304 | tf_op jit(solution)/shard_map/all_to_all | solution.py:680
  54.0 36.0 %collective-permute-start = (f32[16,64,128]{2,1,0:T(8,128)}, f32[16,64,128]{2,1,0:T(8,128)S(1)}, u32[]{:S(2)}, u32[]{:S(2)}) collective-permute-start(f32[16,64,128]{2,1,0:T(8,128)} %get-tuple-element.95), channel_id=1, source_target_pairs={{0,4},{1,5},{2,6},{3,7},{4,0},{5,1},{6,2},{7,3},{8,12},{9,13},{10,... | collective-permute-start | bytes 1572872 | tf_op jit(solution)/shard_map/ppermute | solution.py:704
  89.5 24.3 %collective-permute-start.4 = (f32[16,64,128]{2,1,0:T(8,128)}, f32[16,64,128]{2,1,0:T(8,128)S(1)}, u32[]{:S(2)}, u32[]{:S(2)}) collective-permute-start(f32[16,64,128]{2,1,0:T(8,128)} %get-tuple-element.107), channel_id=1, source_target_pairs={{0,4},{1,5},{2,6},{3,7},{4,0},{5,1},{6,2},{7,3},{8,12},{9,13},{10,... | collective-permute-start | bytes 1572872 | tf_op jit(solution)/shard_map/ppermute | solution.py:704
  93.2 25.3 %collective-permute-start.1 = (f32[16,16,128]{2,1,0:T(8,128)}, f32[16,16,128]{2,1,0:T(8,128)S(1)}, u32[]{:S(2)}, u32[]{:S(2)}) collective-permute-start(f32[16,16,128]{2,1,0:T(8,128)} %get-tuple-element.104), channel_id=1, source_target_pairs={{0,8},{8,0},{16,24},{24,16},{1,9},{9,1},{17,25},{25,17},{2,10},{10... | collective-permute-start | bytes 393224 | tf_op jit(solution)/shard_map/ppermute | solution.py:686
  93.2 25.6 %collective-permute-start.2 = (f32[16,16,128]{2,1,0:T(8,128)}, f32[16,16,128]{2,1,0:T(8,128)S(1)}, u32[]{:S(2)}, u32[]{:S(2)}) collective-permute-start(f32[16,16,128]{2,1,0:T(8,128)} %get-tuple-element.105), channel_id=1, source_target_pairs={{0,16},{8,24},{16,0},{24,8},{1,17},{9,25},{17,1},{25,9},{2,18},{10... | collective-permute-start | bytes 393224 | tf_op jit(solution)/shard_map/ppermute | solution.py:686
  94.8 24.0 %collective-permute-start.3 = (f32[16,16,128]{2,1,0:T(8,128)}, f32[16,16,128]{2,1,0:T(8,128)S(1)}, u32[]{:S(2)}, u32[]{:S(2)}) collective-permute-start(f32[16,16,128]{2,1,0:T(8,128)} %get-tuple-element.106), channel_id=1, source_target_pairs={{0,24},{8,16},{16,8},{24,0},{1,25},{9,17},{17,9},{25,1},{2,26},{10... | collective-permute-start | bytes 393224 | tf_op jit(solution)/shard_map/ppermute | solution.py:686
  116.9 1.9 collective-permute-start.5
  116.9 6.6 %collective-permute-start.6 = (f32[16,16,128]{2,1,0:T(8,128)}, f32[16,16,128]{2,1,0:T(8,128)S(1)}, u32[]{:S(2)}, u32[]{:S(2)}) collective-permute-start(f32[16,16,128]{2,1,0:T(8,128)} %get-tuple-element.113), channel_id=1, source_target_pairs={{0,16},{8,24},{16,0},{24,8},{1,17},{9,25},{17,1},{25,9},{2,18},{10... | collective-permute-start | bytes 393224 | tf_op jit(solution)/shard_map/ppermute | solution.py:686
  118.5 6.9 %copy-start.20 = (f32[16,16,128]{2,1,0:T(8,128)}, f32[16,16,128]{2,1,0:T(8,128)S(1)}, u32[]{:S(2)}) copy-start(f32[16,16,128]{2,1,0:T(8,128)S(1)} %collective-permute-done.1.refs_1_.refs_9_) | copy-start | bytes 393220
  118.5 6.9 %collective-permute-start.7 = (f32[16,16,128]{2,1,0:T(8,128)}, f32[16,16,128]{2,1,0:T(8,128)S(1)}, u32[]{:S(2)}, u32[]{:S(2)}) collective-permute-start(f32[16,16,128]{2,1,0:T(8,128)} %get-tuple-element.114), channel_id=1, source_target_pairs={{0,24},{8,16},{16,8},{24,0},{1,25},{9,17},{17,9},{25,1},{2,26},{10... | collective-permute-start | bytes 393224 | tf_op jit(solution)/shard_map/ppermute | solution.py:686
  118.8 6.6 %copy-start.21 = (f32[16,16,128]{2,1,0:T(8,128)}, f32[16,16,128]{2,1,0:T(8,128)S(1)}, u32[]{:S(2)}) copy-start(f32[16,16,128]{2,1,0:T(8,128)S(1)} %collective-permute-done.2.refs_2_.refs_10_) | copy-start | bytes 393220
  118.8 6.6 %copy-start.22 = (f32[16,16,128]{2,1,0:T(8,128)}, f32[16,16,128]{2,1,0:T(8,128)S(1)}, u32[]{:S(2)}) copy-start(f32[16,16,128]{2,1,0:T(8,128)S(1)} %collective-permute-done.3.refs_3_.refs_11_) | copy-start | bytes 393220
  118.8 6.6 %copy-start.17 = (f32[16,16,128]{2,1,0:T(8,128)}, f32[16,16,128]{2,1,0:T(8,128)S(1)}, u32[]{:S(2)}) copy-start(f32[16,16,128]{2,1,0:T(8,128)S(1)} %collective-permute-done.5.refs_5_.refs_9_) | copy-start | bytes 393220
  132.0 1.9 collective-permute-start.8
  132.3 6.5 %collective-permute-start.9 = (f32[16,16,128]{2,1,0:T(8,128)}, f32[16,16,128]{2,1,0:T(8,128)S(1)}, u32[]{:S(2)}, u32[]{:S(2)}) collective-permute-start(f32[16,16,128]{2,1,0:T(8,128)} %get-tuple-element.118), channel_id=1, source_target_pairs={{0,16},{8,24},{16,0},{24,8},{1,17},{9,25},{17,1},{25,9},{2,18},{10... | collective-permute-start | bytes 393224 | tf_op jit(solution)/shard_map/ppermute | solution.py:686
  133.8 6.5 %collective-permute-start.10 = (f32[16,16,128]{2,1,0:T(8,128)}, f32[16,16,128]{2,1,0:T(8,128)S(1)}, u32[]{:S(2)}, u32[]{:S(2)}) collective-permute-start(f32[16,16,128]{2,1,0:T(8,128)} %get-tuple-element.119), channel_id=1, source_target_pairs={{0,24},{8,16},{16,8},{24,0},{1,25},{9,17},{17,9},{25,1},{2,26},{10... | collective-permute-start | bytes 393224 | tf_op jit(solution)/shard_map/ppermute | solution.py:686
  141.2 25.6 %collective-permute-start.11 = (f32[4,16,16,128]{3,2,1,0:T(8,128)S(1)}, f32[4,16,16,128]{3,2,1,0:T(8,128)S(1)}, u32[]{:S(2)}, u32[]{:S(2)}) collective-permute-start(f32[4,16,16,128]{3,2,1,0:T(8,128)S(1)} %pad_maximum_fusion.refs_0_), channel_id=1, source_target_pairs={{0,4},{1,5},{2,6},{3,7},{4,0},{5,1},{6,2},{7,3},{8,12},{9,13},{10,... | collective-permute-start | bytes 1572872 | tf_op jit(solution)/shard_map/ppermute | solution.py:712
  147.3 3.6 collective-permute-start.12
  147.9 6.6 %collective-permute-start.13 = (f32[16,16,128]{2,1,0:T(8,128)}, f32[16,16,128]{2,1,0:T(8,128)S(1)}, u32[]{:S(2)}, u32[]{:S(2)}) collective-permute-start(f32[16,16,128]{2,1,0:T(8,128)} %get-tuple-element.124), channel_id=1, source_target_pairs={{0,16},{8,24},{16,0},{24,8},{1,17},{9,25},{17,1},{25,9},{2,18},{10... | collective-permute-start | bytes 393224 | tf_op jit(solution)/shard_map/ppermute | solution.py:686
  149.4 6.1 %collective-permute-start.14 = (f32[16,16,128]{2,1,0:T(8,128)}, f32[16,16,128]{2,1,0:T(8,128)S(1)}, u32[]{:S(2)}, u32[]{:S(2)}) collective-permute-start(f32[16,16,128]{2,1,0:T(8,128)} %get-tuple-element.125), channel_id=1, source_target_pairs={{0,24},{8,16},{16,8},{24,0},{1,25},{9,17},{17,9},{25,1},{2,26},{10... | collective-permute-start | bytes 393224 | tf_op jit(solution)/shard_map/ppermute | solution.py:686
  170.3 41.6 %all-to-all-start.2 = ((f32[4,2,16,32,128]{4,3,2,1,0:T(8,128)}), f32[4,2,16,32,128]{4,3,2,1,0:T(8,128)S(1)}, u32[]{:S(2)}, u32[]{:S(2)}) async-start(f32[4,2,16,32,128]{4,3,2,1,0:T(8,128)} %get-tuple-element.126), calls=%async_computation.2 | async-start | bytes 4194304 | tf_op jit(solution)/shard_map/all_to_all | solution.py:680
  174.0 34.4 %collective-permute-start.15 = (f32[4,16,16,128]{3,2,1,0:T(8,128)S(1)}, f32[4,16,16,128]{3,2,1,0:T(8,128)S(1)}, u32[]{:S(2)}, u32[]{:S(2)}) collective-permute-start(f32[4,16,16,128]{3,2,1,0:T(8,128)S(1)} %copy-done.9), channel_id=1, source_target_pairs={{0,4},{1,5},{2,6},{3,7},{4,0},{5,1},{6,2},{7,3},{8,12},{9,13},{10,... | collective-permute-start | bytes 1572872 | tf_op jit(solution)/shard_map/ppermute | solution.py:712
  211.9 6.6 %copy-start.32 = (bf16[2,128,192]{2,1,0:T(8,128)(2,1)S(1)}, bf16[2,128,192]{2,1,0:T(8,128)(2,1)}, u32[]{:S(2)}) copy-start(bf16[2,128,192]{2,1,0:T(8,128)(2,1)} %constant.65.clone) | copy-start | bytes 294916
  213.2 35.0 %all-to-all-start.4 = ((f32[4,2,16,32,128]{4,3,2,1,0:T(8,128)}), f32[4,2,16,32,128]{4,3,2,1,0:T(8,128)}, u32[]{:S(2)}, u32[]{:S(2)}) async-start(f32[4,2,16,32,128]{4,3,2,1,0:T(8,128)} %get-tuple-element.131), calls=%async_computation.4 | async-start | bytes 4194304 | tf_op jit(solution)/shard_map/all_to_all | solution.py:680
  248.1 33.7 %all-to-all-start.3 = ((f32[4,2,16,32,128]{4,3,2,1,0:T(8,128)}), f32[4,2,16,32,128]{4,3,2,1,0:T(8,128)S(1)}, u32[]{:S(2)}, u32[]{:S(2)}) async-start(f32[4,2,16,32,128]{4,3,2,1,0:T(8,128)} %bitcast.38), calls=%async_computation.3 | async-start | bytes 4194304 | tf_op jit(solution)/shard_map/all_to_all | solution.py:680
  283.2 38.9 %all-to-all-start.5 = ((f32[4,2,16,32,128]{4,3,2,1,0:T(8,128)}), f32[4,2,16,32,128]{4,3,2,1,0:T(8,128)S(1)}, u32[]{:S(2)}, u32[]{:S(2)}) async-start(f32[4,2,16,32,128]{4,3,2,1,0:T(8,128)} %bitcast.37), calls=%async_computation.5 | async-start | bytes 4194304 | tf_op jit(solution)/shard_map/all_to_all | solution.py:680
  289.7 36.5 %collective-permute-start.16 = (f32[16,64,128]{2,1,0:T(8,128)}, f32[16,64,128]{2,1,0:T(8,128)S(1)}, u32[]{:S(2)}, u32[]{:S(2)}) collective-permute-start(f32[16,64,128]{2,1,0:T(8,128)} %get-tuple-element.135), channel_id=1, source_target_pairs={{0,4},{1,5},{2,6},{3,7},{4,0},{5,1},{6,2},{7,3},{8,12},{9,13},{10,... | collective-permute-start | bytes 1572872 | tf_op jit(solution)/shard_map/ppermute | solution.py:704
  325.7 23.9 %collective-permute-start.20 = (f32[16,64,128]{2,1,0:T(8,128)}, f32[16,64,128]{2,1,0:T(8,128)S(1)}, u32[]{:S(2)}, u32[]{:S(2)}) collective-permute-start(f32[16,64,128]{2,1,0:T(8,128)} %get-tuple-element.147), channel_id=1, source_target_pairs={{0,4},{1,5},{2,6},{3,7},{4,0},{5,1},{6,2},{7,3},{8,12},{9,13},{10,... | collective-permute-start | bytes 1572872 | tf_op jit(solution)/shard_map/ppermute | solution.py:704
  329.3 25.3 %collective-permute-start.17 = (f32[16,16,128]{2,1,0:T(8,128)}, f32[16,16,128]{2,1,0:T(8,128)S(1)}, u32[]{:S(2)}, u32[]{:S(2)}) collective-permute-start(f32[16,16,128]{2,1,0:T(8,128)} %get-tuple-element.144), channel_id=1, source_target_pairs={{0,8},{8,0},{16,24},{24,16},{1,9},{9,1},{17,25},{25,17},{2,10},{10... | collective-permute-start | bytes 393224 | tf_op jit(solution)/shard_map/ppermute | solution.py:686
  329.4 25.3 %collective-permute-start.18 = (f32[16,16,128]{2,1,0:T(8,128)}, f32[16,16,128]{2,1,0:T(8,128)S(1)}, u32[]{:S(2)}, u32[]{:S(2)}) collective-permute-start(f32[16,16,128]{2,1,0:T(8,128)} %get-tuple-element.145), channel_id=1, source_target_pairs={{0,16},{8,24},{16,0},{24,8},{1,17},{9,25},{17,1},{25,9},{2,18},{10... | collective-permute-start | bytes 393224 | tf_op jit(solution)/shard_map/ppermute | solution.py:686
  330.9 23.8 %collective-permute-start.19 = (f32[16,16,128]{2,1,0:T(8,128)}, f32[16,16,128]{2,1,0:T(8,128)S(1)}, u32[]{:S(2)}, u32[]{:S(2)}) collective-permute-start(f32[16,16,128]{2,1,0:T(8,128)} %get-tuple-element.146), channel_id=1, source_target_pairs={{0,24},{8,16},{16,8},{24,0},{1,25},{9,17},{17,9},{25,1},{2,26},{10... | collective-permute-start | bytes 393224 | tf_op jit(solution)/shard_map/ppermute | solution.py:686
  352.7 2.0 collective-permute-start.21
  353.1 6.6 %collective-permute-start.22 = (f32[16,16,128]{2,1,0:T(8,128)}, f32[16,16,128]{2,1,0:T(8,128)S(1)}, u32[]{:S(2)}, u32[]{:S(2)}) collective-permute-start(f32[16,16,128]{2,1,0:T(8,128)} %get-tuple-element.155), channel_id=1, source_target_pairs={{0,16},{8,24},{16,0},{24,8},{1,17},{9,25},{17,1},{25,9},{2,18},{10... | collective-permute-start | bytes 393224 | tf_op jit(solution)/shard_map/ppermute | solution.py:686
  354.7 6.2 %copy-start.10 = (f32[16,16,128]{2,1,0:T(8,128)}, f32[16,16,128]{2,1,0:T(8,128)S(1)}, u32[]{:S(2)}) copy-start(f32[16,16,128]{2,1,0:T(8,128)S(1)} %collective-permute-done.17.refs_1_) | copy-start | bytes 393220
  354.7 6.2 %collective-permute-start.23 = (f32[16,16,128]{2,1,0:T(8,128)}, f32[16,16,128]{2,1,0:T(8,128)S(1)}, u32[]{:S(2)}, u32[]{:S(2)}) collective-permute-start(f32[16,16,128]{2,1,0:T(8,128)} %get-tuple-element.156), channel_id=1, source_target_pairs={{0,24},{8,16},{16,8},{24,0},{1,25},{9,17},{17,9},{25,1},{2,26},{10... | collective-permute-start | bytes 393224 | tf_op jit(solution)/shard_map/ppermute | solution.py:686
  354.7 6.2 %copy-start.11 = (f32[16,16,128]{2,1,0:T(8,128)}, f32[16,16,128]{2,1,0:T(8,128)S(1)}, u32[]{:S(2)}) copy-start(f32[16,16,128]{2,1,0:T(8,128)S(1)} %collective-permute-done.18.refs_2_) | copy-start | bytes 393220
  367.1 2.2 collective-permute-start.28
  367.7 6.6 %collective-permute-start.29 = (f32[16,16,128]{2,1,0:T(8,128)}, f32[16,16,128]{2,1,0:T(8,128)S(1)}, u32[]{:S(2)}, u32[]{:S(2)}) collective-permute-start(f32[16,16,128]{2,1,0:T(8,128)} %get-tuple-element.165), channel_id=1, source_target_pairs={{0,16},{8,24},{16,0},{24,8},{1,17},{9,25},{17,1},{25,9},{2,18},{10... | collective-permute-start | bytes 393224 | tf_op jit(solution)/shard_map/ppermute | solution.py:686
  369.2 6.1 %collective-permute-start.30 = (f32[16,16,128]{2,1,0:T(8,128)}, f32[16,16,128]{2,1,0:T(8,128)S(1)}, u32[]{:S(2)}, u32[]{:S(2)}) collective-permute-start(f32[16,16,128]{2,1,0:T(8,128)} %get-tuple-element.166), channel_id=1, source_target_pairs={{0,24},{8,16},{16,8},{24,0},{1,25},{9,17},{17,9},{25,1},{2,26},{10... | collective-permute-start | bytes 393224 | tf_op jit(solution)/shard_map/ppermute | solution.py:686
  376.3 8.1 %copy-start.7 = (f32[4,16,16,128]{3,2,1,0:T(8,128)}, f32[4,16,16,128]{3,2,1,0:T(8,128)S(1)}, u32[]{:S(2)}) copy-start(f32[4,16,16,128]{3,2,1,0:T(8,128)S(1)} %pad_maximum_fusion.3.refs_13_.refs_0_) | copy-start | bytes 1572868
  376.3 26.7 %collective-permute-start.31 = (f32[4,16,16,128]{3,2,1,0:T(8,128)S(1)}, f32[4,16,16,128]{3,2,1,0:T(8,128)S(1)}, u32[]{:S(2)}, u32[]{:S(2)}) collective-permute-start(f32[4,16,16,128]{3,2,1,0:T(8,128)S(1)} %pad_maximum_fusion.3.refs_13_.refs_0_), channel_id=1, source_target_pairs={{0,4},{1,5},{2,6},{3,7},{4,0},{5,1},{6,2},{7,3},{8,12},{9,13},{10,... | collective-permute-start | bytes 1572872 | tf_op jit(solution)/shard_map/ppermute | solution.py:712
  384.4 2.0 collective-permute-start.24
  384.8 6.6 %collective-permute-start.25 = (f32[16,16,128]{2,1,0:T(8,128)}, f32[16,16,128]{2,1,0:T(8,128)S(1)}, u32[]{:S(2)}, u32[]{:S(2)}) collective-permute-start(f32[16,16,128]{2,1,0:T(8,128)} %get-tuple-element.161), channel_id=1, source_target_pairs={{0,16},{8,24},{16,0},{24,8},{1,17},{9,25},{17,1},{25,9},{2,18},{10... | collective-permute-start | bytes 393224 | tf_op jit(solution)/shard_map/ppermute | solution.py:686
  386.4 6.2 %collective-permute-start.26 = (f32[16,16,128]{2,1,0:T(8,128)}, f32[16,16,128]{2,1,0:T(8,128)S(1)}, u32[]{:S(2)}, u32[]{:S(2)}) collective-permute-start(f32[16,16,128]{2,1,0:T(8,128)} %get-tuple-element.162), channel_id=1, source_target_pairs={{0,24},{8,16},{16,8},{24,0},{1,25},{9,17},{17,9},{25,1},{2,26},{10... | collective-permute-start | bytes 393224 | tf_op jit(solution)/shard_map/ppermute | solution.py:686
  406.5 41.3 %all-to-all-start.7 = ((f32[4,2,16,32,128]{4,3,2,1,0:T(8,128)}), f32[4,2,16,32,128]{4,3,2,1,0:T(8,128)S(1)}, u32[]{:S(2)}, u32[]{:S(2)}) async-start(f32[4,2,16,32,128]{4,3,2,1,0:T(8,128)} %get-tuple-element.171), calls=%async_computation.7 | async-start | bytes 4194304 | tf_op jit(solution)/shard_map/all_to_all | solution.py:680
  410.2 34.2 %collective-permute-start.27 = (f32[4,16,16,128]{3,2,1,0:T(8,128)S(1)}, f32[4,16,16,128]{3,2,1,0:T(8,128)S(1)}, u32[]{:S(2)}, u32[]{:S(2)}) collective-permute-start(f32[4,16,16,128]{3,2,1,0:T(8,128)S(1)} %copy-done.8), channel_id=1, source_target_pairs={{0,4},{1,5},{2,6},{3,7},{4,0},{5,1},{6,2},{7,3},{8,12},{9,13},{10,... | collective-permute-start | bytes 1572872 | tf_op jit(solution)/shard_map/ppermute | solution.py:712
  449.2 29.9 %all-to-all-start.6 = ((f32[4,2,16,32,128]{4,3,2,1,0:T(8,128)}), f32[4,2,16,32,128]{4,3,2,1,0:T(8,128)S(1)}, u32[]{:S(2)}, u32[]{:S(2)}) async-start(f32[4,2,16,32,128]{4,3,2,1,0:T(8,128)} %get-tuple-element.170), calls=%async_computation.6 | async-start | bytes 4194304 | tf_op jit(solution)/shard_map/all_to_all | solution.py:680
  (26 other events, 57.1 us)
